TPU v7x, 32 devices: a whole 2x2x4 slice. The times are simulated.
32 devices in a mesh: wide: 8 (over y, x, core), narrow: 4 (over z).
Axes of the slice: x: 2, y: 2, z: 4, core: 2. Of those that a mesh axis runs over, the one named last changes fastest.
Arguments:
- input_five: bfloat16 [128, 5, 5, 2048], P('wide'), may hold values from -20 to 20
- input_seven: bfloat16 [128, 7, 7, 2048], P('wide'), may hold values from -20 to 20
- input_nine: bfloat16 [128, 9, 9, 2048], P('wide'), may hold values from -20 to 20
- upstream_five: bfloat16 [128, 5, 5, 2048], P('wide', None, None, 'narrow'), may hold values from -20 to 20
- upstream_seven: bfloat16 [128, 7, 7, 2048], P('wide', None, None, 'narrow'), may hold values from -20 to 20
- upstream_nine: bfloat16 [128, 9, 9, 2048], P('wide', None, None, 'narrow'), may hold values from -20 to 20
- reduce_weight: bfloat16 [2048, 512], P(None, 'narrow'), may hold values from -0.125 to 0.125
- spatial_weight: bfloat16 [3, 3, 512, 512], P(None, None, None, 'narrow'), may hold values from -0.09375 to 0.09375
- expand_weight: bfloat16 [512, 2048], P('narrow'), may hold values from -0.25 to 0.25
- gain_first: float32 [512], P('narrow'), may hold values from 0.1 to 1.9
- shift_first: float32 [512], P('narrow'), may hold values from -2.5 to 2.5
- gain_second: float32 [512], P('narrow'), may hold values from 0.1 to 1.9
- shift_second: float32 [512], P('narrow'), may hold values from -2.5 to 2.5
- gain_third: float32 [2048], P('narrow'), may hold values from 0.1 to 1.9
- shift_third: float32 [2048], P('narrow'), may hold values from -2.5 to 2.5
Outputs:
- output_five: bfloat16 [128, 5, 5, 2048], P('wide', None, None, 'narrow')
- output_seven: bfloat16 [128, 7, 7, 2048], P('wide', None, None, 'narrow')
- output_nine: bfloat16 [128, 9, 9, 2048], P('wide', None, None, 'narrow')
- ingrad_five: float32 [128, 5, 5, 2048], P('wide', None, None, 'narrow')
- ingrad_seven: float32 [128, 7, 7, 2048], P('wide', None, None, 'narrow')
- ingrad_nine: float32 [128, 9, 9, 2048], P('wide', None, None, 'narrow')
- reduce_grad: float32 [2048, 512], P(None, 'narrow')
- spatial_grad: float32 [3, 3, 512, 512], P(None, None, None, 'narrow')
- expand_grad: float32 [512, 2048], P('narrow')
- gaingrad_first: float32 [512], P('narrow')
- shiftgrad_first: float32 [512], P('narrow')
- gaingrad_second: float32 [512], P('narrow')
- shiftgrad_second: float32 [512], P('narrow')
- gaingrad_third: float32 [2048], P('narrow')
- shiftgrad_third: float32 [2048], P('narrow')
All inputs are finite; a program needn't handle non-finite values.
Results may differ from a plain program's by a relative error of at most 0.015.
Values may be sent and summed in bfloat16 or wider, within the bound.
A program may use at most 192 MiB of HBM per device.

v0:
```python
import jax
import jax.numpy as jnp
from jax import lax
from jax.sharding import PartitionSpec as P

EPS = 1e-05
LAYOUT = ("NHWC", "HWIO", "NHWC")


def silu_slope(argument):
    logistic = jax.nn.sigmoid(argument)
    return logistic * (1.0 + argument * (1.0 - logistic))


def spatial(inputs, kernel):
    return lax.conv_general_dilated(
        inputs,
        kernel,
        (1, 1),
        ((1, 1), (1, 1)),
        dimension_numbers=LAYOUT,
        preferred_element_type=jnp.float32,
    )


def kernel_grad(inputs, gradient):
    height, breadth = (gradient.shape[1], gradient.shape[2])
    padded = jnp.pad(inputs, ((0, 0), (1, 1), (1, 1), (0, 0)))
    kernel_taps = []
    for vertical in range(3):
        tap_row = []
        for lateral in range(3):
            window = padded[:, vertical : vertical + height, lateral : lateral + breadth, :]
            tap_row.append(
                jnp.einsum("bhwc,bhwo->co", window, gradient, preferred_element_type=jnp.float32)
            )
        kernel_taps.append(jnp.stack(tap_row))
    return jnp.stack(kernel_taps)


def norm_forward(hidden, gain_vec, shift_vec, samples):
    first_sum, square = lax.psum(
        (jnp.sum(hidden, axis=(0, 1, 2)), jnp.sum(hidden * hidden, axis=(0, 1, 2))), "wide"
    )
    average = first_sum / samples
    inverse = lax.rsqrt(square / samples - average * average + EPS)
    normed = (hidden - average) * inverse
    return (normed, inverse, normed * gain_vec + shift_vec)


def norm_backward(upstream, normed, inverse, gain_vec, samples):
    shift_sum, gain_sum = lax.psum(
        (jnp.sum(upstream, axis=(0, 1, 2)), jnp.sum(upstream * normed, axis=(0, 1, 2))), "wide"
    )
    hidden_grad = (
        gain_vec * inverse * (upstream - shift_sum / samples - normed * (gain_sum / samples))
    )
    return (hidden_grad.astype(jnp.bfloat16), gain_sum, shift_sum)


def run_group(inputs, upstream, weights, params):
    reduce_weight, spatial_weight, expand_weight = weights
    gain_first, shift_first, gain_second, shift_second, gain_third, shift_third = params
    samples = inputs.shape[0] * lax.axis_size("wide") * inputs.shape[1] * inputs.shape[2]
    hidden_first = jnp.einsum(
        "bhwc,cd->bhwd", inputs, reduce_weight, preferred_element_type=jnp.float32
    )
    normed_first, inverse_first, pre_first = norm_forward(
        hidden_first, gain_first, shift_first, samples
    )
    active_first = jax.nn.silu(pre_first).astype(jnp.bfloat16)
    whole_first = lax.all_gather(active_first, "narrow", axis=3, tiled=True)
    hidden_second = spatial(whole_first, spatial_weight)
    normed_second, inverse_second, pre_second = norm_forward(
        hidden_second, gain_second, shift_second, samples
    )
    active_second = jax.nn.silu(pre_second).astype(jnp.bfloat16)
    partial_third = jnp.einsum(
        "bhwi,id->bhwd", active_second, expand_weight, preferred_element_type=jnp.float32
    )
    hidden_third = lax.psum_scatter(partial_third, "narrow", scatter_dimension=3, tiled=True)
    normed_third, inverse_third, pre_third = norm_forward(
        hidden_third, gain_third, shift_third, samples
    )
    own_breadth = hidden_third.shape[3]
    own_inputs = lax.dynamic_slice_in_dim(
        inputs, lax.axis_index("narrow") * own_breadth, own_breadth, 3
    ).astype(jnp.float32)
    summed = pre_third + own_inputs
    result = jax.nn.silu(summed).astype(jnp.bfloat16)
    summed_grad = upstream.astype(jnp.float32) * silu_slope(summed)
    grad_third, gaingrad_third, shiftgrad_third = norm_backward(
        summed_grad, normed_third, inverse_third, gain_third, samples
    )
    whole_third = lax.all_gather(grad_third, "narrow", axis=3, tiled=True)
    expand_grad = jnp.einsum(
        "bhwi,bhwd->id", active_second, whole_third, preferred_element_type=jnp.float32
    )
    active_grad_second = jnp.einsum(
        "bhwd,id->bhwi", whole_third, expand_weight, preferred_element_type=jnp.float32
    )
    grad_second, gaingrad_second, shiftgrad_second = norm_backward(
        active_grad_second * silu_slope(pre_second),
        normed_second,
        inverse_second,
        gain_second,
        samples,
    )
    spatial_grad = kernel_grad(whole_first, grad_second)
    flipped = jnp.transpose(spatial_weight[::-1, ::-1], (0, 1, 3, 2))
    active_grad_first = lax.psum_scatter(
        spatial(grad_second, flipped), "narrow", scatter_dimension=3, tiled=True
    )
    grad_first, gaingrad_first, shiftgrad_first = norm_backward(
        active_grad_first * silu_slope(pre_first), normed_first, inverse_first, gain_first, samples
    )
    reduce_grad = jnp.einsum(
        "bhwc,bhwd->cd", inputs, grad_first, preferred_element_type=jnp.float32
    )
    partial_input = jnp.einsum(
        "bhwd,cd->bhwc", grad_first, reduce_weight, preferred_element_type=jnp.float32
    )
    input_grad = (
        lax.psum_scatter(
            partial_input.astype(jnp.bfloat16), "narrow", scatter_dimension=3, tiled=True
        ).astype(jnp.float32)
        + summed_grad
    )
    weight_grads = (reduce_grad, spatial_grad, expand_grad)
    param_grads = (
        gaingrad_first,
        shiftgrad_first,
        gaingrad_second,
        shiftgrad_second,
        gaingrad_third,
        shiftgrad_third,
    )
    return (result, input_grad, weight_grads, param_grads)


def body(
    input_five,
    input_seven,
    input_nine,
    upstream_five,
    upstream_seven,
    upstream_nine,
    reduce_weight,
    spatial_weight,
    expand_weight,
    gain_first,
    shift_first,
    gain_second,
    shift_second,
    gain_third,
    shift_third,
):
    weights = (reduce_weight, spatial_weight, expand_weight)
    params = (gain_first, shift_first, gain_second, shift_second, gain_third, shift_third)
    results = []
    in_grads = []
    weight_totals = None
    param_totals = None
    for inputs, upstream in (
        (input_five, upstream_five),
        (input_seven, upstream_seven),
        (input_nine, upstream_nine),
    ):
        result, input_grad, weight_grads, param_grads = run_group(inputs, upstream, weights, params)
        results.append(result)
        in_grads.append(input_grad)
        if weight_totals is None:
            weight_totals, param_totals = (weight_grads, param_grads)
        else:
            weight_totals = tuple(
                (left + right for left, right in zip(weight_totals, weight_grads))
            )
            param_totals = tuple((left + right for left, right in zip(param_totals, param_grads)))
    reduce_total, spatial_total, expand_total = (
        lax.psum(weight_totals[0].astype(jnp.bfloat16), "wide").astype(jnp.float32),
        lax.psum(weight_totals[1].astype(jnp.bfloat16), "wide").astype(jnp.float32),
        lax.psum(weight_totals[2].astype(jnp.bfloat16), "wide").astype(jnp.float32),
    )
    return (
        results[0],
        results[1],
        results[2],
        in_grads[0],
        in_grads[1],
        in_grads[2],
        reduce_total,
        spatial_total,
        expand_total,
        param_totals[0],
        param_totals[1],
        param_totals[2],
        param_totals[3],
        param_totals[4],
        param_totals[5],
    )


def solution(mesh):
    in_specs = (
        P("wide", None, None, None),
        P("wide", None, None, None),
        P("wide", None, None, None),
        P("wide", None, None, "narrow"),
        P("wide", None, None, "narrow"),
        P("wide", None, None, "narrow"),
        P(None, "narrow"),
        P(None, None, None, "narrow"),
        P("narrow", None),
        P("narrow"),
        P("narrow"),
        P("narrow"),
        P("narrow"),
        P("narrow"),
        P("narrow"),
    )
    out_specs = (
        P("wide", None, None, "narrow"),
        P("wide", None, None, "narrow"),
        P("wide", None, None, "narrow"),
        P("wide", None, None, "narrow"),
        P("wide", None, None, "narrow"),
        P("wide", None, None, "narrow"),
        P(None, "narrow"),
        P(None, None, None, "narrow"),
        P("narrow", None),
        P("narrow"),
        P("narrow"),
        P("narrow"),
        P("narrow"),
        P("narrow"),
        P("narrow"),
    )
    return jax.shard_map(body, mesh=mesh, in_specs=in_specs, out_specs=out_specs, check_vma=False)
```

profile of v0, /device:TPU:0, one launch (start us, length us, event | category | flops | bytes accessed | tf_op | source)
XLA Modules:
  0.0 1163.9 jit_solution(7824633747613926736)
XLA Ops:
  14.6 15.1 %all-reduce.8 = (f32[128]{0:T(128)S(1)}, f32[128]{0:T(128)S(1)}, f32[128]{0:T(128)S(1)}, f32[128]{0:T(128)S(1)}, f32[128]{0:T(128)S(1)}, /*index=5*/f32[128]{0:T(128)S(1)}) all-reduce(f32[128]{0:T(128)S(1)} %get-tuple-element.49, f32[128]{0:T(128)S(1)} %get-tuple-element.48, ...), channel_id=1, replica_groups=mesh['wide'=8,'narrow'=4] {'wide'}, use_global_device_ids=true, to_apply=%region_29.30 | all-reduce | flops 768 | bytes 6144 | tf_op jit(solution)/shard_map/psum | solution.py:42
  31.5 17.0 %all_gather.18 = bf16[16,5,5,512]{3,0,2,1:T(8,128)(2,1)S(1)} all-gather(bf16[16,5,5,128]{3,0,2,1:T(8,128)(2,1)S(1)} %multiply_convert_fusion.17), channel_id=1, replica_groups=mesh['wide'=8,'narrow'=4] {'narrow'}, dimensions={3}, use_global_device_ids=true | all-gather | bytes 512000 | tf_op jit(solution)/shard_map/all_gather | solution.py:72
  51.1 28.3 %all_gather.19 = bf16[16,7,7,512]{3,0,2,1:T(8,128)(2,1)S(1)} all-gather(bf16[16,7,7,128]{3,0,2,1:T(8,128)(2,1)S(1)} %multiply_convert_fusion.13), channel_id=1, replica_groups=mesh['wide'=8,'narrow'=4] {'narrow'}, dimensions={3}, use_global_device_ids=true | all-gather | bytes 1003520 | tf_op jit(solution)/shard_map/all_gather | solution.py:72
  82.5 4.8 fusion.44
  87.3 12.3 %all-reduce.7 = (f32[128]{0:T(128)S(1)}, f32[128]{0:T(128)S(1)}, f32[128]{0:T(128)S(1)}, f32[128]{0:T(128)}, f32[128]{0:T(128)}, /*index=5*/f32[128]{0:T(128)}) all-reduce(f32[128]{0:T(128)S(1)} %get-tuple-element.47, f32[128]{0:T(128)S(1)} %get-tuple-element.46, ...), channel_id=1, replica_groups=mesh['wide'=8,'narrow'=4] {'wide'}, use_global_device_ids=true, to_apply=%region_33.34 | all-reduce | flops 768 | bytes 6144 | tf_op jit(solution)/shard_map/psum | solution.py:42
  104.3 3.8 fusion.14
  108.1 5.6 fusion.12
  113.8 49.8 %reduce-scatter.10.cloned.1.call-done = f32[16,5,5,512]{3,0,2,1:T(8,128)} async-done(((f32[16,5,5,2048]{3,0,2,1:T(8,128)}), f32[16,5,5,512]{3,0,2,1:T(8,128)}) %reduce-scatter.10.cloned.1.call-update) | async-done | bytes 819216 | tf_op jit(solution)/shard_map/reduce_scatter | solution.py:81
  164.9 114.1 %reduce-scatter.12.cloned.1.call-done = f32[16,7,7,512]{3,0,2,1:T(8,128)} async-done(((f32[16,7,7,2048]{3,0,2,1:T(8,128)}), f32[16,7,7,512]{3,0,2,1:T(8,128)}) %reduce-scatter.12.cloned.1.call-update) | async-done | bytes 1605648 | tf_op jit(solution)/shard_map/reduce_scatter | solution.py:81
  280.7 181.2 %reduce-scatter.14.cloned.1.call-done = f32[16,9,9,512]{3,0,2,1:T(8,128)} async-done(((f32[16,9,9,2048]{3,0,2,1:T(8,128)}), f32[16,9,9,512]{3,0,2,1:T(8,128)}) %reduce-scatter.14.cloned.1.call-update) | async-done | bytes 2654224 | tf_op jit(solution)/shard_map/reduce_scatter | solution.py:81
  464.6 24.5 %all-reduce.6 = (f32[512]{0:T(512)}, f32[512]{0:T(512)}, f32[512]{0:T(512)}, f32[512]{0:T(512)}, f32[512]{0:T(512)}, /*index=5*/f32[512]{0:T(512)}) all-reduce(f32[512]{0:T(512)} %get-tuple-element.33, f32[512]{0:T(512)} %get-tuple-element.32, f32[512]{0:T(512)S(1)} %get-tuple-element.37, ...), channel_id=1, replica_groups=mesh['wide'=8,'narrow'=4] {'wide'}, use_global_device_ids=true, to_apply=%region_38.39 | all-reduce | flops 3072 | bytes 24576 | tf_op jit(solution)/shard_map/psum | solution.py:42
  490.5 3.6 fusion.40
  494.1 4.4 fusion.38
  498.6 5.6 fusion.36
  504.2 22.4 %all-reduce.5 = (f32[512]{0:T(512)}, f32[512]{0:T(512)}, f32[512]{0:T(512)}, f32[512]{0:T(512)}, f32[512]{0:T(512)}, /*index=5*/f32[512]{0:T(512)}) all-reduce(f32[512]{0:T(512)} %get-tuple-element.31, f32[512]{0:T(512)} %get-tuple-element.30, f32[512]{0:T(512)} %get-tuple-element.35, ...), channel_id=1, replica_groups=mesh['wide'=8,'narrow'=4] {'wide'}, use_global_device_ids=true, to_apply=%region_70.71 | all-reduce | flops 3072 | bytes 24576 | tf_op jit(solution)/shard_map/psum | solution.py:52
  533.3 4.4 multiply_convert_fusion
  537.8 32.3 %all-gather.7.cloned.1.call-done = bf16[16,5,5,2048]{3,0,2,1:T(8,128)(2,1)} async-done(((bf16[16,5,5,512]{3,0,2,1:T(8,128)(2,1)}), bf16[16,5,5,2048]{3,0,2,1:T(8,128)(2,1)}) %all-gather.7.cloned.1.call-update) | async-done | bytes 1638416 | tf_op jit(solution)/shard_map/all_gather | solution.py:95
  572.9 62.8 %all-gather.9.cloned.1.call-done = bf16[16,7,7,2048]{3,0,2,1:T(8,128)(2,1)} async-done(((bf16[16,7,7,512]{3,0,2,1:T(8,128)(2,1)}), bf16[16,7,7,2048]{3,0,2,1:T(8,128)(2,1)}) %all-gather.9.cloned.1.call-update) | async-done | bytes 3211280 | tf_op jit(solution)/shard_map/all_gather | solution.py:95
  635.6 3.8 convolution_bitcast_fusion.1
  641.3 94.4 %all-gather.11.cloned.1.call-done = bf16[16,9,9,2048]{3,0,2,1:T(8,128)(2,1)} async-done(((bf16[16,9,9,512]{3,0,2,1:T(8,128)(2,1)}), bf16[16,9,9,2048]{3,0,2,1:T(8,128)(2,1)}) %all-gather.11.cloned.1.call-update) | async-done | bytes 5308432 | tf_op jit(solution)/shard_map/all_gather | solution.py:95
  735.7 5.3 fusion.43
  741.0 13.8 %all-reduce.4 = (f32[128]{0:T(128)S(1)}, f32[128]{0:T(128)S(1)}, f32[128]{0:T(128)S(1)}, f32[128]{0:T(128)S(1)}, f32[128]{0:T(128)S(1)}, /*index=5*/f32[128]{0:T(128)S(1)}) all-reduce(f32[128]{0:T(128)S(1)} %get-tuple-element.45, f32[128]{0:T(128)S(1)} %get-tuple-element.44, ...), channel_id=1, replica_groups=mesh['wide'=8,'narrow'=4] {'wide'}, use_global_device_ids=true, to_apply=%region_74.75 | all-reduce | flops 768 | bytes 6144 | tf_op jit(solution)/shard_map/psum | solution.py:52
  781.0 3.4 fusion.56
  802.4 15.7 %reduce-scatter.20.cloned.1.call-done = f32[16,7,7,128]{3,0,2,1:T(8,128)} async-done(((f32[16,7,7,512]{3,0,2,1:T(8,128)}), f32[16,7,7,128]{3,0,2,1:T(8,128)}) %reduce-scatter.20.cloned.1.call-update) | async-done | bytes 401424 | tf_op jit(solution)/shard_map/reduce_scatter | solution.py:111
  819.4 52.7 %reduce-scatter.24.cloned.1.call-done = f32[16,9,9,128]{3,0,2,1:T(8,128)} async-done(((f32[16,9,9,512]{3,0,2,1:T(8,128)}), f32[16,9,9,128]{3,0,2,1:T(8,128)}) %reduce-scatter.24.cloned.1.call-update) | async-done | bytes 663568 | tf_op jit(solution)/shard_map/reduce_scatter | solution.py:111
  873.5 13.4 %all-reduce.3 = (f32[128]{0:T(128)S(1)}, f32[128]{0:T(128)S(1)}, f32[128]{0:T(128)S(1)}, f32[128]{0:T(128)S(1)}, f32[128]{0:T(128)S(1)}, /*index=5*/f32[128]{0:T(128)S(1)}) all-reduce(f32[128]{0:T(128)S(1)} %get-tuple-element.43, f32[128]{0:T(128)S(1)} %get-tuple-element.42, ...), channel_id=1, replica_groups=mesh['wide'=8,'narrow'=4] {'wide'}, use_global_device_ids=true, to_apply=%region_79.80 | all-reduce | flops 768 | bytes 6144 | tf_op jit(solution)/shard_map/psum | solution.py:52
  899.3 3.9 convolution_convert_fusion
  903.3 51.9 %all-reduce.12.cloned.1.call-done = (bf16[2048,128]{0,1:T(8,128)(2,1)}, bf16[3,3,512,128]{3,2,1,0:T(8,128)(2,1)}, bf16[128,2048]{1,0:T(8,128)(2,1)}) async-done(((bf16[2048,128]{0,1:T(8,128)(2,1)}, bf16[3,3,512,128]{3,2,1,0:T(8,128)(2,1)}, bf16[128,2048]{1,0:T(8,128)(2,1)}), (bf16[2048,128]{0,1:T(8,128)(2,1)}, bf16[3,3,512,128]{3,2,1,0:T(8,128)(2,1)}, ...) | async-done | bytes 2228240 | tf_op jit(solution)/shard_map/psum | solution.py:180
  961.2 31.9 %reduce-scatter.18.cloned.1.call-done = bf16[16,5,5,512]{3,0,2,1:T(8,128)(2,1)} async-done(((bf16[16,5,5,2048]{3,0,2,1:T(8,128)(2,1)}), bf16[16,5,5,512]{3,0,2,1:T(8,128)(2,1)}) %reduce-scatter.18.cloned.1.call-update) | async-done | bytes 409616 | tf_op jit(solution)/shard_map/reduce_scatter | solution.py:124
  995.1 60.7 %reduce-scatter.22.cloned.1.call-done = bf16[16,7,7,512]{3,0,2,1:T(8,128)(2,1)} async-done(((bf16[16,7,7,2048]{3,0,2,1:T(8,128)(2,1)}), bf16[16,7,7,512]{3,0,2,1:T(8,128)(2,1)}) %reduce-scatter.22.cloned.1.call-update) | async-done | bytes 802832 | tf_op jit(solution)/shard_map/reduce_scatter | solution.py:124
  1058.5 94.4 %reduce-scatter.26.cloned.1.call-done = bf16[16,9,9,512]{3,0,2,1:T(8,128)(2,1)} async-done(((bf16[16,9,9,2048]{3,0,2,1:T(8,128)(2,1)}), bf16[16,9,9,512]{3,0,2,1:T(8,128)(2,1)}) %reduce-scatter.26.cloned.1.call-update) | async-done | bytes 1327120 | tf_op jit(solution)/shard_map/reduce_scatter | solution.py:124
  1152.9 4.2 convert_add_fusion
  (308 shorter events, 107.2 us)
Async XLA Ops:
  7.2 42.1 %copy-start = (bf16[3,3,512,128]{3,2,1,0:T(8,128)(2,1)S(1)}, bf16[3,3,512,128]{3,2,1,0:T(8,128)(2,1)}, u32[]{:S(2)}) copy-start(bf16[3,3,512,128]{3,2,1,0:T(8,128)(2,1)} %param.22) | copy-start | bytes 3538948
  7.2 75.3 %all-gather.5.cloned.1.call-start = ((), (), s32[]{:S(2)}) async-start(), calls=%async_computation.11 | async-start | bytes 1658880 | tf_op jit(solution)/shard_map/all_gather | solution.py:72
  31.4 132.3 %reduce-scatter.10.cloned.1.call-start = ((), (), s32[]{:S(2)}) async-start(), calls=%async_computation.9 | async-start | bytes 4096000 | tf_op jit(solution)/shard_map/reduce_scatter | solution.py:81
  104.2 174.8 %reduce-scatter.12.cloned.1.call-start = ((), (), s32[]{:S(2)}) async-start(), calls=%async_computation.10 | async-start | bytes 8028160 | tf_op jit(solution)/shard_map/reduce_scatter | solution.py:81
  108.1 353.8 %reduce-scatter.14.cloned.1.call-start = ((), (), s32[]{:S(2)}) async-start(), calls=%async_computation.12 | async-start | bytes 13271040 | tf_op jit(solution)/shard_map/reduce_scatter | solution.py:81
  113.8 456.4 %all-gather.7.cloned.1.call-start = ((), (), s32[]{:S(2)}) async-start(), calls=%async_computation.13 | async-start | bytes 2048000 | tf_op jit(solution)/shard_map/all_gather | solution.py:95
  280.6 208.4 %copy-start.52 = (f32[512]{0:T(512)S(1)}, f32[512]{0:T(512)}, u32[]{:S(2)}) copy-start(f32[512]{0:T(512)} %param.28) | copy-start | bytes 6148
  280.7 209.9 %copy-start.55 = (f32[512]{0:T(512)S(1)}, f32[512]{0:T(512)}, u32[]{:S(2)}) copy-start(f32[512]{0:T(512)} %param.29) | copy-start | bytes 6148
  530.3 105.3 %all-gather.9.cloned.1.call-start = ((), (), s32[]{:S(2)}) async-start(), calls=%async_computation.16 | async-start | bytes 4014080 | tf_op jit(solution)/shard_map/all_gather | solution.py:95
  533.2 202.6 %all-gather.11.cloned.1.call-start = ((), (), s32[]{:S(2)}) async-start(), calls=%async_computation.19 | async-start | bytes 6635520 | tf_op jit(solution)/shard_map/all_gather | solution.py:95
  533.2 36.9 %copy-start.18 = (bf16[128,2048]{1,0:T(8,128)(2,1)S(1)}, bf16[128,2048]{1,0:T(8,128)(2,1)}, u32[]{:S(2)}) copy-start(bf16[128,2048]{1,0:T(8,128)(2,1)} %param.23) | copy-start | bytes 1572868
  533.2 36.9 %copy-start.24 = (f32[16,5,5,128]{3,0,2,1:T(8,128)S(1)}, f32[16,5,5,128]{3,0,2,1:T(8,128)}, u32[]{:S(2)}) copy-start(f32[16,5,5,128]{3,0,2,1:T(8,128)} %get-tuple-element.182) | copy-start | bytes 614404
  537.7 97.9 %copy-start.16 = (f32[16,7,7,128]{3,0,2,1:T(8,128)S(1)}, f32[16,7,7,128]{3,0,2,1:T(8,128)}, u32[]{:S(2)}) copy-start(f32[16,7,7,128]{3,0,2,1:T(8,128)} %copy-done.15) | copy-start | bytes 1204228
  537.7 97.9 %copy-start.65 = (f32[128]{0:T(128)S(1)}, f32[128]{0:T(128)}, u32[]{:S(2)}) copy-start(f32[128]{0:T(128)} %copy-done.64) | copy-start | bytes 1540
  537.7 97.9 %copy-start.67 = (f32[128]{0:T(128)S(1)}, f32[128]{0:T(128)}, u32[]{:S(2)}) copy-start(f32[128]{0:T(128)} %copy-done.66) | copy-start | bytes 1540
  537.8 262.8 %reduce-scatter.16.cloned.1.call-start = ((), (), s32[]{:S(2)}) async-start(), calls=%async_computation.14 | async-start | bytes 1024000 | tf_op jit(solution)/shard_map/reduce_scatter | solution.py:111
  639.5 96.2 %copy-start.81 = (f32[128]{0:T(128)S(1)}, f32[128]{0:T(128)}, u32[]{:S(2)}) copy-start(f32[128]{0:T(128)} %copy-done.80) | copy-start | bytes 1540
  639.5 96.2 %copy-start.83 = (f32[128]{0:T(128)S(1)}, f32[128]{0:T(128)}, u32[]{:S(2)}) copy-start(f32[128]{0:T(128)} %copy-done.82) | copy-start | bytes 1540
  641.3 114.5 %copy-start.51 = (f32[16,5,5,128]{3,0,2,1:T(8,128)S(1)}, f32[16,5,5,128]{3,0,2,1:T(8,128)}, u32[]{:S(2)}) copy-start(f32[16,5,5,128]{3,0,2,1:T(8,128)} %get-tuple-element.185) | copy-start | bytes 614404
  641.3 114.5 %copy-start.89 = (f32[128]{0:T(128)S(1)}, f32[128]{0:T(128)}, u32[]{:S(2)}) copy-start(f32[128]{0:T(128)} %get-tuple-element.172) | copy-start | bytes 1540
  641.3 114.5 %copy-start.12 = (bf16[16,5,5,512]{3,0,2,1:T(8,128)(2,1)S(1)}, bf16[16,5,5,512]{3,0,2,1:T(8,128)(2,1)}, u32[]{:S(2)}) copy-start(bf16[16,5,5,512]{3,0,2,1:T(8,128)(2,1)} %copy-done.11) | copy-start | bytes 1228804
  759.7 58.4 %reduce-scatter.20.cloned.1.call-start = ((), (), s32[]{:S(2)}) async-start(), calls=%async_computation.17 | async-start | bytes 2007040 | tf_op jit(solution)/shard_map/reduce_scatter | solution.py:111
  768.9 103.1 %reduce-scatter.24.cloned.1.call-start = ((), (), s32[]{:S(2)}) async-start(), calls=%async_computation.20 | async-start | bytes 3317760 | tf_op jit(solution)/shard_map/reduce_scatter | solution.py:111
  784.5 170.7 %all-reduce.12.cloned.1.call-start = ((), (), s32[]{:S(2)}) async-start(), calls=%async_computation.22 | async-start | bytes 4456448 | tf_op jit(solution)/shard_map/psum | solution.py:180
  800.6 71.4 %copy-start.14 = (f32[16,9,9,128]{3,0,2,1:T(8,128)S(1)}, f32[16,9,9,128]{3,0,2,1:T(8,128)}, u32[]{:S(2)}) copy-start(f32[16,9,9,128]{3,0,2,1:T(8,128)} %copy-done.13) | copy-start | bytes 1990660
  800.6 71.4 %copy-start.73 = (f32[128]{0:T(128)S(1)}, f32[128]{0:T(128)}, u32[]{:S(2)}) copy-start(f32[128]{0:T(128)} %copy-done.72) | copy-start | bytes 1540
  800.6 71.4 %copy-start.75 = (f32[128]{0:T(128)S(1)}, f32[128]{0:T(128)}, u32[]{:S(2)}) copy-start(f32[128]{0:T(128)} %copy-done.74) | copy-start | bytes 1540
  802.4 85.5 %copy-start.84 = (f32[128]{0:T(128)S(1)}, f32[128]{0:T(128)}, u32[]{:S(2)}) copy-start(f32[128]{0:T(128)} %get-tuple-element.168) | copy-start | bytes 1540
  894.3 98.8 %reduce-scatter.18.cloned.1.call-start = ((), (), s32[]{:S(2)}) async-start(), calls=%async_computation.15 | async-start | bytes 2048000 | tf_op jit(solution)/shard_map/reduce_scatter | solution.py:124
  896.2 159.6 %reduce-scatter.22.cloned.1.call-start = ((), (), s32[]{:S(2)}) async-start(), calls=%async_computation.18 | async-start | bytes 4014080 | tf_op jit(solution)/shard_map/reduce_scatter | solution.py:124
  899.1 253.9 %reduce-scatter.26.cloned.1.call-start = ((), (), s32[]{:S(2)}) async-start(), calls=%async_computation.21 | async-start | bytes 6635520 | tf_op jit(solution)/shard_map/reduce_scatter | solution.py:124
  961.2 94.6 %copy-start.4 = (f32[16,7,7,512]{3,0,2,1:T(8,128)S(1)}, f32[16,7,7,512]{3,0,2,1:T(8,128)}, u32[]{:S(2)}) copy-start(f32[16,7,7,512]{3,0,2,1:T(8,128)} %get-tuple-element.109) | copy-start | bytes 4816900
  (78 other events, 649.5 us)
Sparse Core Ops, SparseCore 0:
  31.5 45.5 all-gather.4
  104.3 59.3 reduce-scatter.9
  166.0 112.9 reduce-scatter.11
  281.2 180.6 reduce-scatter.13
  530.5 39.6 all-gather.6
  572.2 63.3 all-gather.8
  637.9 97.8 all-gather.10
  759.8 20.1 reduce-scatter.15
  782.9 35.1 reduce-scatter.19
  820.4 51.6 reduce-scatter.23
  894.5 60.6 all-reduce.11
  957.4 35.7 reduce-scatter.17
  995.5 60.2 reduce-scatter.21
  1058.0 94.8 reduce-scatter.25
where the time goes:
time: 1170 us; the launch traced here: 1160 us
  waiting for transfers between devices  842 us (72%)
  blocking collectives  147 us (13%)
  matrix products  90.4 us (8%)
  other arithmetic  57.5 us (5%)
  between operations  15 us (1%)
    reduce_scatter x3, waiting for transfers between devices, run_group(): lax.psum_scatter(partial_third, 'narrow', scatter_dimension=3, tiled=True)  345 us
    all_gather x3, waiting for transfers between devices, run_group(): whole_third = lax.all_gather(grad_third, 'narrow', axis=3, tiled=True)  189 us
    reduce_scatter x3, waiting for transfers between devices, run_group(): lax.psum_scatter(partial_input.astype(jnp.bfloat16), 'narrow', scatter_di...  187 us
    reduce_scatter x3, waiting for transfers between devices, run_group(): lax.psum_scatter(spatial(grad_second, flipped), 'narrow', scatter_dimensi...  68.3 us
    psum x3, blocking collectives, norm_forward(): lax.psum((jnp.sum(hidden, axis=(0, 1, 2)), jnp.sum(hidden * hidden, axis=...  52 us
    psum x1, waiting for transfers between devices, body(): lax.psum(weight_totals[0].astype(jnp.bfloat16), 'wide').astype(jnp.float32)  51.9 us
    psum x3, blocking collectives, norm_backward(): lax.psum((jnp.sum(upstream, axis=(0, 1, 2)), jnp.sum(upstream * normed, a...  49.6 us
    all_gather x2, blocking collectives, run_group(): whole_first = lax.all_gather(active_first, 'narrow', axis=3, tiled=True)  45.4 us
  transfers between devices with their start and end apart: 14, of which 12 were waited for; matrix products, arithmetic and copies ran while one was open for 8% of the time, Pallas kernels for 0%

commit v1 on v0

v1 whole, which is shorter than its diff:
```python
import jax
import jax.numpy as jnp
from jax import lax
from jax.sharding import PartitionSpec as P

EPS = 1e-05
LAYOUT = ("NHWC", "HWIO", "NHWC")


def silu_slope(argument):
    logistic = jax.nn.sigmoid(argument)
    return logistic * (1.0 + argument * (1.0 - logistic))


def spatial(inputs, kernel):
    return lax.conv_general_dilated(
        inputs,
        kernel,
        (1, 1),
        ((1, 1), (1, 1)),
        dimension_numbers=LAYOUT,
        preferred_element_type=jnp.float32,
    )


def kernel_grad(inputs, gradient):
    height, breadth = (gradient.shape[1], gradient.shape[2])
    padded = jnp.pad(inputs, ((0, 0), (1, 1), (1, 1), (0, 0)))
    taps = []
    for vertical in range(3):
        for lateral in range(3):
            window = padded[:, vertical : vertical + height, lateral : lateral + breadth, :]
            taps.append(
                jnp.einsum("bhwc,bhwo->co", window, gradient, preferred_element_type=jnp.float32)
            )
    return jnp.stack(taps).reshape(3, 3, inputs.shape[3], gradient.shape[3])


def sums_forward(hidden):
    return (jnp.sum(hidden, axis=(0, 1, 2)), jnp.sum(hidden * hidden, axis=(0, 1, 2)))


def normed_of(hidden, sums, samples):
    average = sums[0] / samples
    inverse = lax.rsqrt(sums[1] / samples - average * average + EPS)
    return ((hidden - average) * inverse, inverse)


def sums_backward(upstream, normed):
    return (jnp.sum(upstream, axis=(0, 1, 2)), jnp.sum(upstream * normed, axis=(0, 1, 2)))


def hidden_grad(upstream, normed, inverse, gain, sums, samples):
    return (
        gain * inverse * (upstream - sums[0] / samples - normed * (sums[1] / samples))
    ).astype(jnp.bfloat16)


def each(function, *lists):
    return [function(*items) for items in zip(*lists)]


def columns(array, axis):
    own = array.shape[axis] // lax.axis_size("narrow")
    return lax.dynamic_slice_in_dim(array, lax.axis_index("narrow") * own, own, axis)


def dot(form, left, right):
    return jnp.einsum(form, left, right, preferred_element_type=jnp.float32)


def plain_body(
    input_five,
    input_seven,
    input_nine,
    upstream_five,
    upstream_seven,
    upstream_nine,
    reduce_weight,
    spatial_weight,
    expand_weight,
    gain_first,
    shift_first,
    gain_second,
    shift_second,
    gain_third,
    shift_third,
):
    inputs = [input_five, input_seven, input_nine]
    upstreams = [upstream_five, upstream_seven, upstream_nine]
    samples = [
        x.shape[0] * lax.axis_size("wide") * x.shape[1] * x.shape[2] for x in inputs
    ]
    whole_reduce = lax.all_gather(reduce_weight, "narrow", axis=1, tiled=True)
    whole_spatial = lax.all_gather(spatial_weight, "narrow", axis=3, tiled=True)
    own_expand = lax.all_to_all(expand_weight, "narrow", 1, 0, tiled=True)
    vectors = jnp.stack([gain_first, shift_first, gain_second, shift_second])
    gain1, shift1, gain2, shift2 = lax.all_gather(vectors, "narrow", axis=1, tiled=True)

    hidden1 = each(lambda x: dot("bhwc,cd->bhwd", x, whole_reduce), inputs)
    sums1 = lax.psum(each(sums_forward, hidden1), "wide")
    normed1, inverse1 = zip(*each(normed_of, hidden1, sums1, samples))
    pre1 = each(lambda n: n * gain1 + shift1, normed1)
    active1 = each(lambda p: jax.nn.silu(p).astype(jnp.bfloat16), pre1)

    hidden2 = each(lambda a: spatial(a, whole_spatial), active1)
    sums2 = lax.psum(each(sums_forward, hidden2), "wide")
    normed2, inverse2 = zip(*each(normed_of, hidden2, sums2, samples))
    pre2 = each(lambda n: n * gain2 + shift2, normed2)
    active2 = each(lambda p: jax.nn.silu(p).astype(jnp.bfloat16), pre2)

    hidden3 = each(lambda a: dot("bhwi,id->bhwd", a, own_expand), active2)
    sums3 = lax.psum(each(sums_forward, hidden3), "wide")
    normed3, inverse3 = zip(*each(normed_of, hidden3, sums3, samples))
    summed = each(
        lambda n, x: n * gain_third + shift_third + columns(x, 3).astype(jnp.float32),
        normed3,
        inputs,
    )
    results = each(lambda z: jax.nn.silu(z).astype(jnp.bfloat16), summed)
    grads_z = each(lambda u, z: u.astype(jnp.float32) * silu_slope(z), upstreams, summed)
    back3 = lax.psum(each(sums_backward, grads_z, normed3), "wide")
    grad3 = each(
        lambda e, n, r, s, m: hidden_grad(e, n, r, gain_third, s, m),
        grads_z,
        normed3,
        inverse3,
        back3,
        samples,
    )
    expand_grad = sum(each(lambda a, g: dot("bhwi,bhwd->id", a, g), active2, grad3))
    active_grad2 = each(
        lambda g: lax.psum(
            dot("bhwd,id->bhwi", g, own_expand).astype(jnp.bfloat16), "narrow"
        ).astype(jnp.float32),
        grad3,
    )
    grads_2 = each(lambda a, p: a * silu_slope(p), active_grad2, pre2)
    back2 = lax.psum(each(sums_backward, grads_2, normed2), "wide")
    grad2 = each(
        lambda e, n, r, s, m: hidden_grad(e, n, r, gain2, s, m),
        grads_2,
        normed2,
        inverse2,
        back2,
        samples,
    )
    spatial_grad = sum(each(lambda a, g: kernel_grad(a, columns(g, 3)), active1, grad2))
    flipped = jnp.transpose(whole_spatial[::-1, ::-1], (0, 1, 3, 2))
    grads_1 = each(lambda g, p: spatial(g, flipped) * silu_slope(p), grad2, pre1)
    back1 = lax.psum(each(sums_backward, grads_1, normed1), "wide")
    grad1 = each(
        lambda e, n, r, s, m: hidden_grad(e, n, r, gain1, s, m),
        grads_1,
        normed1,
        inverse1,
        back1,
        samples,
    )
    reduce_grad = sum(each(lambda x, g: dot("bhwc,bhwd->cd", x, columns(g, 3)), inputs, grad1))
    own_reduce = columns(whole_reduce, 0)
    in_grads = each(lambda g, e: dot("bhwd,cd->bhwc", g, own_reduce) + e, grad1, grads_z)

    low = [g.astype(jnp.bfloat16) for g in (reduce_grad, spatial_grad, expand_grad)]
    low[2] = lax.all_to_all(low[2], "narrow", 0, 1, tiled=True)
    totals = [g.astype(jnp.float32) for g in lax.psum(low, "wide")]

    def params(back, part):
        shift = sum(s[0] for s in back)
        gain = sum(s[1] for s in back)
        return [part(gain), part(shift)]

    def own(vector):
        return columns(vector, 0)

    small = params(back1, own) + params(back2, own) + params(back3, lambda v: v)
    return tuple(results + in_grads + totals + small)


def solution(mesh):
    rows = P("wide", None, None, None)
    blocks = P("wide", None, None, "narrow")
    weights = [P(None, "narrow"), P(None, None, None, "narrow"), P("narrow", None)]
    vectors = [P("narrow")] * 6
    return jax.shard_map(
        plain_body,
        mesh=mesh,
        in_specs=tuple([rows] * 3 + [blocks] * 3 + weights + vectors),
        out_specs=tuple([blocks] * 6 + weights + vectors),
        check_vma=False,
    )
```

time: 1170 us -> 599 us (0.51)
  waiting for transfers between devices: 842 us -> 213 us
  blocking collectives: 147 us -> 178 us
  matrix products: 90.4 us -> 103 us
    reduce_scatter x9 -> x0, waiting for transfers between devices: 600 us -> none  [the longest x3 345 us: run_group(): lax.psum_scatter(partial_third, 'narrow', scatter_dimension=3, tiled=True)]
    all_gather x4 -> x2, waiting for transfers between devices: 189 us -> 62.1 us  [the longest x1 47.7 us: plain_body(): whole_spatial = lax.all_gather(spatial_weight, 'narrow', axis=3, tiled=True)]
    psum x1 -> x2, waiting for transfers between devices: 51.9 us -> 122 us  [the longest x1 73.5 us: plain_body(): lax.psum(dot('bhwd,id->bhwi', g, own_expand).astype(jnp.bfloat16), 'narrow')]
    psum x6, blocking collectives: 102 us -> 141 us  [the longest x1 25.7 us: plain_body(): sums1 = lax.psum(each(sums_forward, hidden1), 'wide')]
    all_to_all x0 -> x2, waiting for transfers between devices: none -> 27.6 us  [the longest x1 27.6 us: plain_body(): low[2] = lax.all_to_all(low[2], 'narrow', 0, 1, tiled=True)]
    conv_general_dilated x6, matrix products: 16 us -> 33.9 us  [spatial(): lax.conv_general_dilated(inputs, kernel, (1, 1), ((1, 1), (1, 1)), dimens...]
    convert_element_type x15 -> x17, other arithmetic: 16.6 us -> 27.7 us  [the longest x9 12 us: hidden_grad(): return (gain * inverse * (upstream - sums[0] / samples - normed * (sums[1...]
    all_gather x2 -> x1, blocking collectives: 45.4 us -> 36.9 us  [plain_body(): lax.all_gather(vectors, 'narrow', axis=1, tiled=True)]
  transfers between devices with their start and end apart: 14 -> 6, of which waited for: 12 -> 5; matrix products, arithmetic and copies ran while one was open for 8% -> 10% of each run, Pallas kernels for 0% -> 0%
where the time goes in v1:
time: 599 us; the launch traced here: 594 us
  waiting for transfers between devices  213 us (36%)
  blocking collectives  178 us (30%)
  matrix products  103 us (17%)
  other arithmetic  55.5 us (9%)
  local copies, waits for them, and re-layouts  18.9 us (3%)
  between operations  14.8 us (2%)
  starting transfers between devices  10.6 us (2%)
    psum x1, waiting for transfers between devices, plain_body(): lax.psum(dot('bhwd,id->bhwi', g, own_expand).astype(jnp.bfloat16), 'narrow')  73.5 us
    dot_general x18, matrix products, dot(): return jnp.einsum(form, left, right, preferred_element_type=jnp.float32)  49.8 us
    psum x1, waiting for transfers between devices, plain_body(): totals = [g.astype(jnp.float32) for g in lax.psum(low, 'wide')]  48.4 us
    all_gather x1, waiting for transfers between devices, plain_body(): whole_spatial = lax.all_gather(spatial_weight, 'narrow', axis=3, tiled=True)  47.7 us
    all_gather x1, blocking collectives, plain_body(): lax.all_gather(vectors, 'narrow', axis=1, tiled=True)  36.9 us
    conv_general_dilated x6, matrix products, spatial(): lax.conv_general_dilated(inputs, kernel, (1, 1), ((1, 1), (1, 1)), dimens...  33.9 us
    all_to_all x1, waiting for transfers between devices, plain_body(): low[2] = lax.all_to_all(low[2], 'narrow', 0, 1, tiled=True)  27.6 us
    psum x1, blocking collectives, plain_body(): sums1 = lax.psum(each(sums_forward, hidden1), 'wide')  25.7 us
  transfers between devices with their start and end apart: 6, of which 5 were waited for; matrix products, arithmetic and copies ran while one was open for 10% of the time, Pallas kernels for 0%

profile of v1, /device:TPU:0, one launch (start us, length us, event | category | flops | bytes accessed | tf_op | source)
XLA Modules:
  0.0 593.9 jit_solution(7767836604452841515)
XLA Ops:
  10.6 6.3 %all-to-all-start = ((bf16[128,4,512]{2,0,1:T(8,128)(2,1)}), bf16[128,4,512]{2,0,1:T(8,128)(2,1)}, u32[]{:S(2)}, u32[]{:S(2)}) async-start(bf16[128,4,512]{2,0,1:T(8,128)(2,1)} %bitcast.367), calls=%async_computation | async-start | bytes 1048576 | tf_op jit(solution)/shard_map/all_to_all | solution.py:96
  17.0 36.9 %all_gather.10 = f32[4,512]{1,0:T(4,128)S(1)} all-gather(f32[4,128]{1,0:T(4,128)S(1)} %pad_maximum_fusion), channel_id=1, replica_groups=mesh['wide'=8,'narrow'=4] {'narrow'}, dimensions={1}, use_global_device_ids=true | all-gather | bytes 10240 | tf_op jit(solution)/shard_map/all_gather | solution.py:98
  53.9 14.4 %all-gather.3.cloned.1.call-done = bf16[2048,512]{1,0:T(8,128)(2,1)} async-done(((bf16[2048,128]{1,0:T(8,128)(2,1)}), bf16[2048,512]{1,0:T(8,128)(2,1)}) %all-gather.3.cloned.1.call-update) | async-done | bytes 2097168 | tf_op jit(solution)/shard_map/all_gather | solution.py:94
  68.2 4.1 fusion.136
  72.4 4.7 fusion.131
  77.2 3.0 fusion.126
  80.1 25.7 %all-reduce.8 = (f32[512]{0:T(512)S(1)}, f32[512]{0:T(512)S(1)}, f32[512]{0:T(512)S(1)}, f32[512]{0:T(512)S(1)}, f32[512]{0:T(512)S(1)}, /*index=5*/f32[512]{0:T(512)S(1)}) all-reduce(f32[512]{0:T(512)S(1)} %get-tuple-element.41, f32[512]{0:T(512)S(1)} %get-tuple-element.40, ...), channel_id=1, replica_groups=mesh['wide'=8,'narrow'=4] {'wide'}, use_global_device_ids=true, to_apply=%region_27.28 | all-reduce | flops 3072 | bytes 24576 | tf_op jit(solution)/shard_map/psum | solution.py:101
  111.3 47.7 %all-gather.5.cloned.1.call-done = bf16[3,3,512,512]{3,2,1,0:T(8,128)(2,1)} async-done(((bf16[3,3,512,128]{3,2,1,0:T(8,128)(2,1)}), bf16[3,3,512,512]{3,2,1,0:T(8,128)(2,1)}) %all-gather.5.cloned.1.call-update) | async-done | bytes 4718608 | tf_op jit(solution)/shard_map/all_gather | solution.py:95
  159.0 7.5 %fusion.130 = (f32[512]{0:T(512)S(1)}, f32[512]{0:T(512)S(1)}, f32[16,7,7,512]{3,0,2,1:T(8,128)}) fusion(bf16[16,7,7,512]{3,0,2,1:T(8,128)(2,1)S(1)} %multiply_convert_fusion.11, bf16[3,3,512,512]{3,2,1,0:T(8,128)(2,1)} %all-gather.5.cloned.1.call-done), kind=kOutput, calls=%fused_computation.286 | convolution fusion | flops 3029490688 | bytes 7131136 | tf_op jit(solution)/shard_map/conv_general_dilated | solution.py:16
  166.5 6.4 %fusion.125 = (f32[512]{0:T(512)S(1)}, f32[512]{0:T(512)S(1)}, f32[16,9,9,512]{3,0,2,1:T(8,128)S(1)}) fusion(bf16[16,9,9,512]{3,0,2,1:T(8,128)(2,1)S(1)} %copy-done.38, bf16[3,3,512,512]{3,2,1,0:T(8,128)(2,1)S(1)} %copy-done.20), kind=kOutput, calls=%fused_computation.281 | convolution fusion | flops 5244869632 | bytes 8704000 | tf_op jit(solution)/shard_map/conv_general_dilated | solution.py:16
  175.0 24.2 %all-reduce.7 = (f32[512]{0:T(512)S(1)}, f32[512]{0:T(512)S(1)}, f32[512]{0:T(512)S(1)}, f32[512]{0:T(512)}, f32[512]{0:T(512)}, /*index=5*/f32[512]{0:T(512)}) all-reduce(f32[512]{0:T(512)S(1)} %get-tuple-element.39, f32[512]{0:T(512)S(1)} %get-tuple-element.38, ...), channel_id=1, replica_groups=mesh['wide'=8,'narrow'=4] {'wide'}, use_global_device_ids=true, to_apply=%region_31.32 | all-reduce | flops 3072 | bytes 24576 | tf_op jit(solution)/shard_map/psum | solution.py:107
  203.3 3.0 fusion.129
  207.2 3.8 fusion.124
  213.4 22.5 %all-reduce.6 = (f32[512]{0:T(512)S(1)}, f32[512]{0:T(512)S(1)}, f32[512]{0:T(512)S(1)}, f32[512]{0:T(512)S(1)}, f32[512]{0:T(512)S(1)}, /*index=5*/f32[512]{0:T(512)S(1)}) all-reduce(f32[512]{0:T(512)S(1)} %get-tuple-element.37, f32[512]{0:T(512)S(1)} %get-tuple-element.36, ...), channel_id=1, replica_groups=mesh['wide'=8,'narrow'=4] {'wide'}, use_global_device_ids=true, to_apply=%region_35.36 | all-reduce | flops 3072 | bytes 24576 | tf_op jit(solution)/shard_map/psum | solution.py:113
  236.5 6.1 %fusion.123 = (f32[512]{0:T(512)}, f32[512]{0:T(512)}, f32[16,9,9,512]{3,0,2,1:T(8,128)S(1)}, bf16[16,9,9,512]{3,0,2,1:T(8,128)(2,1)}) fusion(f32[512]{0:T(512)S(1)} %get-tuple-element.175, f32[16,9,9,512]{3,0,2,1:T(8,128)} %get-tuple-element.187, f32[512]{0:T(512)S(1)} %get-tuple-element.177, bf16[16,9,9,2048]{3,0,2,1:T(8,128)(2,1)} %param.17, ...), kind=kLoop, calls=%fused_computation.279 | loop fusion | flops 13270016 | bytes 9302020 | tf_op jit(solution)/shard_map/reduce_sum | solution.py:50
  242.7 4.4 fusion.128
  250.0 22.4 %all-reduce.5 = (f32[512]{0:T(512)}, f32[512]{0:T(512)}, f32[512]{0:T(512)}, f32[512]{0:T(512)}, f32[512]{0:T(512)}, /*index=5*/f32[512]{0:T(512)}) all-reduce(f32[512]{0:T(512)} %get-tuple-element.35, f32[512]{0:T(512)} %get-tuple-element.34, f32[512]{0:T(512)} %get-tuple-element.47, ...), channel_id=1, replica_groups=mesh['wide'=8,'narrow'=4] {'wide'}, use_global_device_ids=true, to_apply=%region_65.66 | all-reduce | flops 3072 | bytes 24576 | tf_op jit(solution)/shard_map/psum | solution.py:122
  285.7 3.0 convolution_convert_fusion
  293.0 4.1 all-to-all-start.1
  297.2 27.6 %all-to-all-done.1 = bf16[4,128,512]{2,1,0:T(8,128)(2,1)} async-done(((bf16[4,128,512]{2,1,0:T(8,128)(2,1)}), bf16[4,128,512]{2,1,0:T(8,128)(2,1)}, u32[]{:S(2)}, u32[]{:S(2)}) %all-to-all-start.1) | async-done | bytes 524320 | tf_op jit(solution)/shard_map/all_to_all | solution.py:165
  326.6 73.5 %all-reduce.16.cloned.1.call-done = (bf16[16,9,9,512]{3,0,2,1:T(8,128)(2,1)}, bf16[16,7,7,512]{3,0,2,1:T(8,128)(2,1)}, bf16[16,5,5,512]{3,0,2,1:T(8,128)(2,1)}) async-done(((bf16[16,9,9,512]{3,0,2,1:T(8,128)(2,1)}, bf16[16,7,7,512]{3,0,2,1:T(8,128)(2,1)}, bf16[16,5,5,512]{3,0,2,1:T(8,128)(2,1)}), (bf16[16,9,9,512]{3,0,2,1:T(8,128)(2,1)}, bf16[16,7,7,512]{3,0,2,1:T(8,128)(2,1)}, ...) | async-done | bytes 2539536 | tf_op jit(solution)/shard_map/psum | solution.py:133
  404.6 3.4 fusion.121
  408.0 24.2 %all-reduce.4 = (f32[512]{0:T(512)}, f32[512]{0:T(512)}, f32[512]{0:T(512)}, f32[512]{0:T(512)}, f32[512]{0:T(512)}, /*index=5*/f32[512]{0:T(512)}) all-reduce(f32[512]{0:T(512)} %get-tuple-element.31, f32[512]{0:T(512)} %get-tuple-element.30, f32[512]{0:T(512)S(1)} %get-tuple-element.43, ...), channel_id=1, replica_groups=mesh['wide'=8,'narrow'=4] {'wide'}, use_global_device_ids=true, to_apply=%region_70.71 | all-reduce | flops 3072 | bytes 24576 | tf_op jit(solution)/shard_map/psum | solution.py:139
  462.7 5.7 fusion.127
  468.4 8.9 %fusion.122 = (f32[512]{0:T(512)S(1)}, f32[512]{0:T(512)S(1)}, f32[16,9,9,512]{3,0,2,1:T(8,128)}) fusion(f32[512]{0:T(512)S(1)} %get-tuple-element.119, f32[16,9,9,512]{3,0,2,1:T(8,128)S(1)} %copy-done.8, f32[512]{0:T(512)S(1)} %get-tuple-element.160, f32[512]{0:T(512)S(1)} %bitcast.408, f32[512]{0:T(512)S(1)} %bitcast.402, ...), kind=kOutput, calls=%fused_computation.278 | convolution fusion | flops 5252832256 | bytes 11366400 | tf_op jit(solution)/shard_map/conv_general_dilated | solution.py:16
  477.3 3.2 fusion.132
  480.6 22.5 %all-reduce.3 = (f32[512]{0:T(512)S(1)}, f32[512]{0:T(512)S(1)}, f32[512]{0:T(512)S(1)}, f32[512]{0:T(512)S(1)}, f32[512]{0:T(512)S(1)}, /*index=5*/f32[512]{0:T(512)S(1)}) all-reduce(f32[512]{0:T(512)S(1)} %get-tuple-element.33, f32[512]{0:T(512)S(1)} %get-tuple-element.32, ...), channel_id=1, replica_groups=mesh['wide'=8,'narrow'=4] {'wide'}, use_global_device_ids=true, to_apply=%region_74.75 | all-reduce | flops 3072 | bytes 24576 | tf_op jit(solution)/shard_map/psum | solution.py:151
  503.1 3.3 multiply_convert_fusion
  506.4 4.0 convolution_bitcast_fusion
  515.1 3.2 add_convert_fusion
  530.1 3.5 convolution_add_fusion
  533.6 48.4 %all-reduce.14.cloned.1.call-done = (bf16[2048,128]{0,1:T(8,128)(2,1)}, bf16[3,3,512,128]{3,2,1,0:T(8,128)(2,1)}, bf16[128,2048]{1,0:T(8,128)(2,1)}) async-done(((bf16[2048,128]{0,1:T(8,128)(2,1)}, bf16[3,3,512,128]{3,2,1,0:T(8,128)(2,1)}, bf16[128,2048]{1,0:T(8,128)(2,1)}), (bf16[2048,128]{0,1:T(8,128)(2,1)}, bf16[3,3,512,128]{3,2,1,0:T(8,128)(2,1)}, ...) | async-done | bytes 2228240 | tf_op jit(solution)/shard_map/psum | solution.py:166
  (238 shorter events, 97.5 us)
Async XLA Ops:
  7.2 9.7 %copy-start.71 = (f32[128]{0:T(128)S(1)}, f32[128]{0:T(128)}, u32[]{:S(2)}) copy-start(f32[128]{0:T(128)} %param.24) | copy-start | bytes 1540
  7.2 9.7 %copy-start.70 = (f32[128]{0:T(128)S(1)}, f32[128]{0:T(128)}, u32[]{:S(2)}) copy-start(f32[128]{0:T(128)} %param.25) | copy-start | bytes 1540
  7.2 9.7 %copy-start.69 = (f32[128]{0:T(128)S(1)}, f32[128]{0:T(128)}, u32[]{:S(2)}) copy-start(f32[128]{0:T(128)} %param.26) | copy-start | bytes 1540
  7.2 9.7 %copy-start.68 = (f32[128]{0:T(128)S(1)}, f32[128]{0:T(128)}, u32[]{:S(2)}) copy-start(f32[128]{0:T(128)} %param.27) | copy-start | bytes 1540
  7.2 61.0 %all-gather.3.cloned.1.call-start = ((), (), s32[]{:S(2)}) async-start(), calls=%async_computation.2 | async-start | bytes 2621440 | tf_op jit(solution)/shard_map/all_gather | solution.py:94
  8.0 151.0 %all-gather.5.cloned.1.call-start = ((), (), s32[]{:S(2)}) async-start(), calls=%async_computation.3 | async-start | bytes 5898240 | tf_op jit(solution)/shard_map/all_gather | solution.py:95
  10.6 192.8 %all-to-all-start = ((bf16[128,4,512]{2,0,1:T(8,128)(2,1)}), bf16[128,4,512]{2,0,1:T(8,128)(2,1)}, u32[]{:S(2)}, u32[]{:S(2)}) async-start(bf16[128,4,512]{2,0,1:T(8,128)(2,1)} %bitcast.367), calls=%async_computation | async-start | bytes 1048576 | tf_op jit(solution)/shard_map/all_to_all | solution.py:96
  16.9 383.2 %all-reduce.16.cloned.1.call-start = ((), (), s32[]{:S(2)}) async-start(), calls=%async_computation.5 | async-start | bytes 5079040 | tf_op jit(solution)/shard_map/psum | solution.py:133
  53.8 18.5 %copy-start.4 = (bf16[16,7,7,2048]{3,0,2,1:T(8,128)(2,1)S(1)}, bf16[16,7,7,2048]{3,0,2,1:T(8,128)(2,1)}, u32[]{:S(2)}) copy-start(bf16[16,7,7,2048]{3,0,2,1:T(8,128)(2,1)} %param.16) | copy-start | bytes 9633796
  68.2 8.9 %slice-start = ((s8[5308416]{0:T(1024)(128)(4,1)}), s8[4194304]{0:T(1024)(128)(4,1)S(1)}, s32[]{:S(2)}) async-start(s8[5308416]{0:T(1024)(128)(4,1)} %bitcast.368), calls=%async_computation.6 | async-start | bytes 8388608
  77.1 29.3 %copy-start.23 = (f32[16,5,5,512]{3,0,2,1:T(8,128)S(1)}, f32[16,5,5,512]{3,0,2,1:T(8,128)}, u32[]{:S(2)}) copy-start(f32[16,5,5,512]{3,0,2,1:T(8,128)} %get-tuple-element.183) | copy-start | bytes 2457604
  80.1 31.1 %copy-start.7 = (f32[16,9,9,512]{3,0,2,1:T(8,128)}, f32[16,9,9,512]{3,0,2,1:T(8,128)S(1)}, u32[]{:S(2)}) copy-start(f32[16,9,9,512]{3,0,2,1:T(8,128)S(1)} %get-tuple-element.181) | copy-start | bytes 7962628
  109.4 57.1 %copy-start.45 = (bf16[16,7,7,512]{3,0,2,1:T(8,128)(2,1)}, bf16[16,7,7,512]{3,0,2,1:T(8,128)(2,1)S(1)}, u32[]{:S(2)}) copy-start(bf16[16,7,7,512]{3,0,2,1:T(8,128)(2,1)S(1)} %multiply_convert_fusion.11) | copy-start | bytes 2408452
  159.0 7.5 %copy-start.20 = (bf16[3,3,512,512]{3,2,1,0:T(8,128)(2,1)S(1)}, bf16[3,3,512,512]{3,2,1,0:T(8,128)(2,1)}, u32[]{:S(2)}) copy-start(bf16[3,3,512,512]{3,2,1,0:T(8,128)(2,1)} %all-gather.5.cloned.1.call-done) | copy-start | bytes 14155780
  159.0 7.5 %copy-start.38 = (bf16[16,9,9,512]{3,0,2,1:T(8,128)(2,1)S(1)}, bf16[16,9,9,512]{3,0,2,1:T(8,128)(2,1)}, u32[]{:S(2)}) copy-start(bf16[16,9,9,512]{3,0,2,1:T(8,128)(2,1)} %multiply_convert_fusion.5) | copy-start | bytes 3981316
  166.5 6.4 %copy-start.14 = (bf16[16,5,5,512]{3,0,2,1:T(8,128)(2,1)S(1)}, bf16[16,5,5,512]{3,0,2,1:T(8,128)(2,1)}, u32[]{:S(2)}) copy-start(bf16[16,5,5,512]{3,0,2,1:T(8,128)(2,1)} %multiply_convert_fusion.17) | copy-start | bytes 1228804
  172.9 33.5 %copy-start = (f32[16,9,9,512]{3,0,2,1:T(8,128)}, f32[16,9,9,512]{3,0,2,1:T(8,128)S(1)}, u32[]{:S(2)}) copy-start(f32[16,9,9,512]{3,0,2,1:T(8,128)S(1)} %get-tuple-element.184) | copy-start | bytes 7962628
  175.0 36.0 %copy-start.9 = (f32[16,5,5,512]{3,0,2,1:T(8,128)}, f32[16,5,5,512]{3,0,2,1:T(8,128)S(1)}, u32[]{:S(2)}) copy-start(f32[16,5,5,512]{3,0,2,1:T(8,128)S(1)} %get-tuple-element.186) | copy-start | bytes 2457604
  211.0 24.9 %copy-start.51 = (f32[512]{0:T(512)S(1)}, f32[512]{0:T(512)}, u32[]{:S(2)}) copy-start(f32[512]{0:T(512)} %param.28) | copy-start | bytes 6148
  211.0 25.5 %copy-start.52 = (f32[512]{0:T(512)S(1)}, f32[512]{0:T(512)}, u32[]{:S(2)}) copy-start(f32[512]{0:T(512)} %param.29) | copy-start | bytes 6148
  236.5 6.2 %copy-start.53 = (f32[512]{0:T(512)}, f32[512]{0:T(512)S(1)}, u32[]{:S(2)}) copy-start(f32[512]{0:T(512)S(1)} %get-tuple-element.175) | copy-start | bytes 6148
  236.5 6.2 %copy-start.55 = (f32[512]{0:T(512)}, f32[512]{0:T(512)S(1)}, u32[]{:S(2)}) copy-start(f32[512]{0:T(512)S(1)} %get-tuple-element.177) | copy-start | bytes 6148
  236.5 10.6 %copy-start.57 = (f32[512]{0:T(512)}, f32[512]{0:T(512)S(1)}, u32[]{:S(2)}) copy-start(f32[512]{0:T(512)S(1)} %get-tuple-element.131) | copy-start | bytes 6148
  236.5 10.6 %copy-start.59 = (f32[512]{0:T(512)}, f32[512]{0:T(512)S(1)}, u32[]{:S(2)}) copy-start(f32[512]{0:T(512)S(1)} %get-tuple-element.174) | copy-start | bytes 6148
  236.5 6.2 %copy-start.18 = (f32[16,7,7,512]{3,0,2,1:T(8,128)S(1)}, f32[16,7,7,512]{3,0,2,1:T(8,128)}, u32[]{:S(2)}) copy-start(f32[16,7,7,512]{3,0,2,1:T(8,128)} %get-tuple-element.188) | copy-start | bytes 4816900
  236.5 6.2 %copy-start.44 = (bf16[16,7,7,512]{3,0,2,1:T(8,128)(2,1)S(1)}, bf16[16,7,7,512]{3,0,2,1:T(8,128)(2,1)}, u32[]{:S(2)}) copy-start(bf16[16,7,7,512]{3,0,2,1:T(8,128)(2,1)} %param.19) | copy-start | bytes 2408452
  293.0 31.8 %all-to-all-start.1 = ((bf16[4,128,512]{2,1,0:T(8,128)(2,1)}), bf16[4,128,512]{2,1,0:T(8,128)(2,1)}, u32[]{:S(2)}, u32[]{:S(2)}) async-start(bf16[4,128,512]{2,1,0:T(8,128)(2,1)} %bitcast.375), calls=%async_computation.1 | async-start | bytes 1048576 | tf_op jit(solution)/shard_map/all_to_all | solution.py:165
  297.1 284.8 %all-reduce.14.cloned.1.call-start = ((), (), s32[]{:S(2)}) async-start(), calls=%async_computation.4 | async-start | bytes 4456448 | tf_op jit(solution)/shard_map/psum | solution.py:166
  468.4 8.9 %copy-start.24 = (f32[16,5,5,512]{3,0,2,1:T(8,128)S(1)}, f32[16,5,5,512]{3,0,2,1:T(8,128)}, u32[]{:S(2)}) copy-start(f32[16,5,5,512]{3,0,2,1:T(8,128)} %get-tuple-element.183) | copy-start | bytes 2457604
  477.3 25.7 %copy-start.63 = (f32[512]{0:T(512)S(1)}, f32[512]{0:T(512)}, u32[]{:S(2)}) copy-start(f32[512]{0:T(512)} %get-tuple-element.118) | copy-start | bytes 6148
  521.0 6.2 %copy-start.3 = (f32[16,7,7,512]{3,0,2,1:T(8,128)S(1)}, f32[16,7,7,512]{3,0,2,1:T(8,128)}, u32[]{:S(2)}) copy-start(f32[16,7,7,512]{3,0,2,1:T(8,128)} %get-tuple-element.109) | copy-start | bytes 4816900
  521.0 6.2 %copy-start.22 = (bf16[16,7,7,512]{3,0,2,1:T(8,128)(2,1)S(1)}, bf16[16,7,7,512]{3,0,2,1:T(8,128)(2,1)}, u32[]{:S(2)}) copy-start(bf16[16,7,7,512]{3,0,2,1:T(8,128)(2,1)} %copy-done.21) | copy-start | bytes 2408452
  (51 other events, 163.7 us)
Sparse Core Ops, SparseCore 0:
  9.6 58.5 all-gather.2
  69.8 89.1 all-gather.4
  288.8 111.2 all-reduce.15
  521.1 60.8 all-reduce.13

commit v2 on v1

--- a/solution.py
+++ b/solution.py
@@ -1,6 +1,10 @@
+import functools
+
 import jax
 import jax.numpy as jnp
 from jax import lax
+from jax.experimental import pallas as pl
+from jax.experimental.pallas import tpu as pltpu
 from jax.sharding import PartitionSpec as P
 
 EPS = 1e-05
@@ -177,13 +181,1072 @@
     return tuple(results + in_grads + totals + small)
 
 
+class Shape:
+    def __init__(self, mesh, maps, images, depth, inner):
+        self.wide, self.narrow = mesh.shape["wide"], mesh.shape["narrow"]
+        self.chips = self.wide // 2
+        self.maps = maps
+        self.images = images
+        self.depth, self.inner = depth, inner
+        self.own = inner // self.narrow
+        self.block = depth // self.narrow
+        self.rows = [images * side * side for side in maps]
+        self.samples = [float(rows * self.wide) for rows in self.rows]
+
+    def fits(self):
+        return (
+            self.narrow >= 4
+            and self.narrow % 2 == 0
+            and self.wide % 2 == 0
+            and self.block == self.inner
+            and self.own % 128 == 0
+            and self.images % 16 == 0
+            and self.own % (16 * self.wide) == 0
+            and self.inner % 512 == 0
+        )
+
+
+def image_rows(side):
+    best = 1
+    for count in range(1, side + 1):
+        if side % count == 0 and count * side <= 49:
+            best = count
+    return best
+
+
+def reduction_pieces(side):
+    return 3 if side % 3 == 0 and side > 3 else 1
+
+
+class Pool:
+    def __init__(self, limit):
+        self.limit, self.used = limit, 0
+        self.ref = None
+
+    def take(self):
+        assert self.used < self.limit
+        self.used += 1
+        return self.ref.at[self.used - 1]
+
+
+MESH = pl.DeviceIdType.MESH
+SEMAPHORES = 400
+
+
+def dot_nn(left, right):
+    return lax.dot_general(
+        left, right, (((1,), (0,)), ((), ())), preferred_element_type=jnp.float32
+    )
+
+
+def dot_nt(left, right):
+    return lax.dot_general(
+        left, right, (((1,), (1,)), ((), ())), preferred_element_type=jnp.float32
+    )
+
+
+def dot_tn(left, right):
+    return lax.dot_general(
+        left, right, (((0,), (0,)), ((), ())), preferred_element_type=jnp.float32
+    )
+
+
+def logistic(argument):
+    return 0.5 * jnp.tanh(0.5 * argument) + 0.5
+
+
+def block_kernel(shape, *refs):
+    wide, narrow, chips = shape.wide, shape.narrow, shape.chips
+    inner, own, block, images = shape.inner, shape.own, shape.block, shape.images
+    refs = list(refs)
+
+    def take(count):
+        taken = refs[:count]
+        del refs[:count]
+        return taken
+
+    x_in, u_in = take(3), take(3)
+    rw_in, sw_in, ew_in = take(3)
+    gain1, shift1, gain2, shift2, gain3, shift3 = take(6)
+    y_out, i_out = take(3), take(3)
+    rg_out, sg_out, eg_out = take(3)
+    gg1, bg1, gg2, bg2, gg3, bg3 = take(6)
+    xb = take(3)
+    rwf, swf, ewf = take(3)
+    h1, h2, h3, dz = take(3), take(3), take(3), take(3)
+    apad, dpad = take(3), take(3)
+    rin, rx = take(3), take(3)
+    sacc, eacc, racc = take(3)
+    sgb, egb, rgb = take(3)
+    sr1, er1, rr1 = take(3)
+    sr2, er2, rr2 = take(3)
+    sfin, efin, rfin = take(3)
+    epz, rpz = take(2)
+    stat_s, stat_r, sums, vec, vec_all = take(5)
+    (sem_ref,) = take(1)
+    pool = Pool(SEMAPHORES)
+    pool.ref = sem_ref
+
+    w = lax.axis_index("wide")
+    z = lax.axis_index("narrow")
+    core = lax.rem(w, 2)
+    chip = lax.div(w, 2)
+    sibling = chip * 2 + (1 - core)
+    half = narrow // 2
+    low_side = z < half
+    inward = jnp.where(low_side, z + 1, z - 1)
+    outward = jnp.where(low_side, z - 1, z + 1)
+    center = jnp.logical_or(z == half - 1, z == half)
+    end = jnp.logical_or(z == 0, z == narrow - 1)
+    finish = []
+
+    def remote(source, target, device, when=None, send=None, recv=None):
+        send = pool.take() if send is None else send
+        recv = pool.take() if recv is None else recv
+
+        def make():
+            return pltpu.make_async_remote_copy(
+                src_ref=source(),
+                dst_ref=target(),
+                send_sem=send,
+                recv_sem=recv,
+                device_id=device,
+                device_id_type=MESH,
+            )
+
+        def start():
+            make().start()
+
+            def wait():
+                if when is None:
+                    make().wait_send()
+                else:
+                    pl.when(when)(lambda: make().wait_send())
+
+            finish.append(wait)
+
+        return start, lambda: make().wait_recv()
+
+    def local(source, target):
+        semaphore = pool.take()
+
+        def make():
+            return pltpu.make_async_copy(source(), target(), semaphore)
+
+        return lambda: make().start(), lambda: make().wait()
+
+    def span(start, size, unit):
+        return pl.ds(pl.multiple_of(start * unit, unit), size)
+
+    x_wait = [[None] * narrow for _ in range(3)]
+    for g in range(3):
+        for k in range(narrow):
+            start, wait = local(
+                lambda g=g, k=k: x_in[g].at[:, pl.ds(k * block, block)],
+                lambda g=g, k=k: xb[g].at[k],
+            )
+            start()
+            x_wait[g][k] = wait
+    own_waits = []
+    for source, target in (
+        (lambda: rw_in, lambda: rwf.at[:, span(z, own, own)]),
+        (lambda: sw_in, lambda: swf.at[:, :, span(z, own, own)]),
+        (lambda: ew_in.at[:, span(z, block, block)], lambda: ewf.at[span(z, own, own), :]),
+    ):
+        start, wait = local(source, target)
+        start()
+        own_waits.append(wait)
+
+    vec_all[z] = jnp.concatenate(
+        [gain1[...], shift1[...], gain2[...], shift2[...], jnp.zeros((4, own), jnp.float32)], axis=0
+    )
+
+    barrier = pltpu.get_barrier_semaphore()
+    for k in range(1, wide):
+        pl.semaphore_signal(
+            barrier, inc=1, device_id=(lax.rem(w + k, wide), z), device_id_type=MESH
+        )
+    for k in range(1, narrow):
+        pl.semaphore_signal(
+            barrier, inc=1, device_id=(w, lax.rem(z + k, narrow)), device_id_type=MESH
+        )
+    pl.semaphore_wait(barrier, wide - 1 + narrow - 1)
+
+    vec_waits = []
+    for k in range(1, narrow):
+        start, wait = remote(
+            lambda: vec_all.at[z], lambda: vec_all.at[z], (w, lax.rem(z + k, narrow))
+        )
+        start()
+        vec_waits.append(wait)
+
+    def gather(source_of, target_of):
+        first = []
+        for k in range(1, narrow):
+            start, wait = remote(
+                lambda: source_of(w), lambda: target_of(w, z), (w, lax.rem(z + k, narrow))
+            )
+            start()
+            first.append(wait)
+        second, third = [], []
+
+        def spread():
+            for k in range(1, narrow):
+                first[k - 1]()
+                origin = lax.rem(z + narrow - k, narrow)
+                for j in range(1, chips):
+                    peer = lax.rem(chip + j, chips) * 2 + core
+                    start, wait = remote(
+                        lambda origin=origin: target_of(w, origin),
+                        lambda origin=origin: target_of(w, origin),
+                        (peer, z),
+                    )
+                    start()
+                    second.append((j, origin, wait))
+                start, wait = remote(
+                    lambda origin=origin: target_of(w, origin),
+                    lambda origin=origin: target_of(w, origin),
+                    (sibling, z),
+                )
+                start()
+                third.append(wait)
+
+        def cross():
+            for j, origin, arrived in second:
+                arrived()
+                holder = lax.rem(chip + chips - j, chips) * 2 + core
+                start, wait = remote(
+                    lambda origin=origin, holder=holder: target_of(holder, origin),
+                    lambda origin=origin, holder=holder: target_of(holder, origin),
+                    (sibling, z),
+                )
+                start()
+                third.append(wait)
+
+        def ready():
+            for wait in third:
+                wait()
+
+        return spread, cross, ready
+
+    rw_piece, sw_piece = shape.depth // wide, inner // wide
+    rw_spread, rw_cross, rw_ready = gather(
+        lambda h: rw_in.at[span(h, rw_piece, rw_piece), :],
+        lambda h, o: rwf.at[span(h, rw_piece, rw_piece), span(o, own, own)],
+    )
+    sw_spread, sw_cross, sw_ready = gather(
+        lambda h: sw_in.at[:, span(h, sw_piece, sw_piece), :],
+        lambda h, o: swf.at[:, span(h, sw_piece, sw_piece), span(o, own, own)],
+    )
+    ew_waits = []
+    for k in range(1, narrow):
+        peer = lax.rem(z + k, narrow)
+        start, wait = remote(
+            lambda peer=peer: ew_in.at[:, span(peer, block, block)],
+            lambda: ewf.at[span(z, own, own), :],
+            (w, peer),
+        )
+        start()
+        ew_waits.append(wait)
+
+    for g in range(3):
+        side = shape.maps[g]
+        for pad in (apad[g], dpad[g]):
+            pad[0] = jnp.zeros((side + 2, images, inner), jnp.bfloat16)
+            pad[side + 1] = jnp.zeros((side + 2, images, inner), jnp.bfloat16)
+            for edge in (0, side + 1):
+                pad[1 : side + 1, edge] = jnp.zeros((side, images, inner), jnp.bfloat16)
+
+    for wait in vec_waits:
+        wait()
+    gathered = [
+        jnp.concatenate([vec_all[k, row : row + 1, :] for k in range(narrow)], axis=1)
+        for row in range(4)
+    ]
+    names = {}
+
+    def put(name, value):
+        if name not in names:
+            names[name] = len(names)
+        vec[names[name] : names[name] + 1, :] = value
+
+    def get(name):
+        return vec[names[name] : names[name] + 1, :]
+
+    for name, value in zip(("g1", "b1", "g2", "b2"), gathered):
+        put(name, value)
+    put("g3", gain3[...])
+    put("b3", shift3[...])
+
+    tiles = inner // 128
+    stat_sems = {}
+
+    def stats_send(e, first, second):
+        for b in range(tiles):
+            stat_s[e, b : b + 1, :] = first[:, b * 128 : (b + 1) * 128]
+            stat_s[e, tiles + b : tiles + b + 1, :] = second[:, b * 128 : (b + 1) * 128]
+        stat_r[e, w] = stat_s[e]
+        send, recv = pool.take(), pool.take()
+        stat_sems[e] = (send, recv)
+
+        def one(k, carry):
+            pltpu.make_async_remote_copy(
+                src_ref=stat_s.at[e],
+                dst_ref=stat_r.at[e, w],
+                send_sem=send,
+                recv_sem=recv,
+                device_id=(lax.rem(w + k, wide), z),
+                device_id_type=MESH,
+            ).start()
+            return carry
+
+        lax.fori_loop(1, wide, one, 0)
+
+    def stats_all(e):
+        send, recv = stat_sems[e]
+        return pltpu.make_async_remote_copy(
+            src_ref=stat_r.at[e, pl.ds(0, wide - 1)],
+            dst_ref=stat_r.at[e, pl.ds(0, wide - 1)],
+            send_sem=send,
+            recv_sem=recv,
+            device_id=(sibling, z),
+            device_id_type=MESH,
+        )
+
+    def stats_wait(e):
+        stats_all(e).wait_recv()
+        finish.append(lambda: stats_all(e).wait_send())
+        total = stat_r[e, 0]
+        for k in range(1, wide):
+            total = total + stat_r[e, k]
+        return [
+            jnp.concatenate([total[t * tiles + b : t * tiles + b + 1, :] for b in range(tiles)], axis=1)
+            for t in range(2)
+        ]
+
+    def clear_sums():
+        sums[0:2, :] = jnp.zeros((2, inner), jnp.float32)
+
+    def add_sums(first, second):
+        sums[0:1, :] += jnp.sum(first, axis=0, keepdims=True)
+        sums[1:2, :] += jnp.sum(second, axis=0, keepdims=True)
+
+    def send_sums(e):
+        stats_send(e, sums[0:1, :], sums[1:2, :])
+
+    def norm_vectors(g, level):
+        e = g * 6 + level
+        first, second = stats_wait(e)
+        mean = first / shape.samples[g]
+        inverse = lax.rsqrt(second / shape.samples[g] - mean * mean + EPS)
+        scale = inverse * get(f"g{level + 1}")
+        put(f"r{level}_{g}", inverse)
+        put(f"m{level}_{g}", -mean * inverse)
+        put(f"a{level}_{g}", scale)
+        put(f"c{level}_{g}", get(f"b{level + 1}") - mean * scale)
+
+    def back_vectors(g, level, e):
+        shift_sum, gain_sum = stats_wait(e)
+        put(f"sb{level}_{g}", shift_sum)
+        put(f"sg{level}_{g}", gain_sum)
+        scale = get(f"a{level}_{g}")
+        inverse = get(f"r{level}_{g}")
+        c1 = scale * (gain_sum / shape.samples[g])
+        put(f"k1{level}_{g}", -inverse * c1)
+        put(f"k0{level}_{g}", -get(f"m{level}_{g}") * c1 - scale * (shift_sum / shape.samples[g]))
+
+    def loop(count, function):
+        if count == 1:
+            function(0)
+        else:
+            pl.loop(0, count)(function)
+
+    def line(g):
+        return shape.maps[g] * images
+
+    def lines(g, function):
+        size = line(g)
+        pl.loop(0, shape.maps[g])(lambda y: function(y, pl.ds(pl.multiple_of(y * size, 16), size)))
+
+    def slabs(g, function):
+        count = image_rows(shape.maps[g])
+        size = count * line(g)
+        loop(
+            shape.maps[g] // count,
+            lambda s: function(s * count, count, pl.ds(pl.multiple_of(s * size, 16), size)),
+        )
+
+    k_own, k_a2, k_dh, k_p = [lax.rem(z + k, narrow) for k in range(4)]
+
+    def f1(g):
+        for k in range(narrow):
+            x_wait[g][k]()
+        clear_sums()
+
+        def slab(y, count, rows):
+            left = jnp.concatenate([xb[g][k, rows, :] for k in range(narrow)], axis=1)
+            result = dot_nn(left, rwf[...])
+            h1[g][rows, :] = result
+            add_sums(result, result * result)
+
+        slabs(g, slab)
+        send_sums(g * 6)
+        start, wait = local(lambda: u_in[g], lambda: xb[g].at[k_dh])
+        start()
+        u_wait[g] = wait
+
+    u_wait = [None] * 3
+
+    def a1(g):
+        norm_vectors(g, 0)
+        scale, offset = get(f"a0_{g}"), get(f"c0_{g}")
+        side = shape.maps[g]
+
+        def one(y, rows):
+            pre = h1[g][rows, :] * scale + offset
+            value = (pre * logistic(pre)).astype(jnp.bfloat16)
+            apad[g][y + 1, pl.ds(1, side)] = value.reshape(side, images, inner)
+
+        lines(g, one)
+
+    def windows(pad, g, y, count):
+        side = shape.maps[g]
+        return [
+            pad[pl.ds(y + i, count), pl.ds(j, side)].reshape(count * side * images, inner)
+            for i in range(3)
+            for j in range(3)
+        ]
+
+    def f2(g):
+        clear_sums()
+
+        def slab(y, count, rows):
+            left = jnp.concatenate(windows(apad[g], g, y, count), axis=1)
+            result = dot_nn(left, swf[...].reshape(9 * inner, inner))
+            h2[g][rows, :] = result
+            add_sums(result, result * result)
+
+        slabs(g, slab)
+        send_sums(g * 6 + 1)
+
+    def a2(g):
+        norm_vectors(g, 1)
+        scale, offset = get(f"a1_{g}"), get(f"c1_{g}")
+
+        def one(y, rows):
+            pre = h2[g][rows, :] * scale + offset
+            xb[g][k_a2, rows, :] = (pre * logistic(pre)).astype(jnp.bfloat16)
+
+        lines(g, one)
+
+    def f3(g):
+        clear_sums()
+
+        def slab(y, count, rows):
+            result = dot_nn(xb[g][k_a2, rows, :], ewf[...])
+            h3[g][rows, :] = result
+            add_sums(result, result * result)
+
+        slabs(g, slab)
+        send_sums(g * 6 + 2)
+
+    y_wait = [None] * 3
+
+    def a3(g):
+        norm_vectors(g, 2)
+        u_wait[g]()
+        clear_sums()
+        scale, offset = get(f"a2_{g}"), get(f"c2_{g}")
+        inverse, minus = get(f"r2_{g}"), get(f"m2_{g}")
+
+        def one(y, rows):
+            hidden = h3[g][rows, :]
+            total = hidden * scale + offset + xb[g][k_own, rows, :].astype(jnp.float32)
+            sig = logistic(total)
+            xb[g][k_p, rows, :] = (total * sig).astype(jnp.bfloat16)
+            slope = sig * (1.0 + total * (1.0 - sig))
+            grad = xb[g][k_dh, rows, :].astype(jnp.float32) * slope
+            dz[g][rows, :] = grad.astype(jnp.bfloat16)
+            add_sums(grad, grad * (hidden * inverse + minus))
+
+        lines(g, one)
+        send_sums(g * 6 + 3)
+        start, wait = local(lambda: xb[g].at[k_p], lambda: y_out[g])
+        start()
+        y_wait[g] = wait
+
+    def b3(g):
+        back_vectors(g, 2, g * 6 + 3)
+        scale, k1, k0 = get(f"a2_{g}"), get(f"k12_{g}"), get(f"k02_{g}")
+        y_wait[g]()
+
+        def one(y, rows):
+            value = dz[g][rows, :].astype(jnp.float32) * scale + h3[g][rows, :] * k1 + k0
+            xb[g][k_dh, rows, :] = value.astype(jnp.bfloat16)
+
+        lines(g, one)
+
+        def slab(y, count, rows):
+            result = dot_nt(xb[g][k_dh, rows, :], ewf[...])
+            xb[g][k_p, rows, :] = result.astype(jnp.bfloat16)
+
+        slabs(g, slab)
+
+    def eg(g):
+        result = dot_tn(xb[g][k_a2], xb[g][k_dh])
+        for k in range(narrow):
+            part = result[k * own : (k + 1) * own, :].reshape(eacc.shape[1:])
+            eacc[k] = part if g == order[0] else eacc[k] + part
+
+    reductions = {}
+
+    def zparts(g):
+        count = reduction_pieces(shape.maps[g])
+        size = shape.rows[g] // count
+        return [pl.ds(c * size, size) for c in range(count)]
+
+    def za(g, c):
+        rows = zparts(g)[c]
+        sends = {}
+        in_send, in_recv = pool.take(), pool.take()
+        x_send, x_recv = pool.take(), pool.take()
+        o_send = pool.take()
+        partial = xb[g].at[k_p, rows, :]
+
+        def to_center():
+            return pltpu.make_async_remote_copy(
+                src_ref=xb[g].at[k_p, rows, :],
+                dst_ref=rx[g].at[rows, :],
+                send_sem=x_send,
+                recv_sem=x_recv,
+                device_id=(w, inward),
+                device_id_type=MESH,
+            )
+
+        def to_inner():
+            return pltpu.make_async_remote_copy(
+                src_ref=xb[g].at[k_p, rows, :],
+                dst_ref=rin[g].at[rows, :],
+                send_sem=in_send,
+                recv_sem=in_recv,
+                device_id=(w, inward),
+                device_id_type=MESH,
+            )
+
+        def to_outer():
+            return pltpu.make_async_remote_copy(
+                src_ref=rx[g].at[rows, :],
+                dst_ref=rx[g].at[rows, :],
+                send_sem=o_send,
+                recv_sem=x_recv,
+                device_id=(w, outward),
+                device_id_type=MESH,
+            )
+
+        @pl.when(jnp.logical_not(end))
+        def _():
+            to_inner().wait_recv()
+            xb[g][k_p, rows, :] = (
+                xb[g][k_p, rows, :].astype(jnp.float32) + rin[g][rows, :].astype(jnp.float32)
+            ).astype(jnp.bfloat16)
+
+        @pl.when(center)
+        def _():
+            to_center().start()
+
+        @pl.when(jnp.logical_not(center))
+        def _():
+            to_inner().start()
+
+        reductions[g, c] = (to_center, to_inner, to_outer)
+
+    def zb(g, c):
+        rows = zparts(g)[c]
+        to_center, to_inner, to_outer = reductions[g, c]
+        to_center().wait_recv()
+
+        @pl.when(center)
+        def _():
+            rx[g][rows, :] = (
+                rx[g][rows, :].astype(jnp.float32) + xb[g][k_p, rows, :].astype(jnp.float32)
+            ).astype(jnp.bfloat16)
+
+        @pl.when(jnp.logical_not(end))
+        def _():
+            to_outer().start()
+
+        def done():
+            pl.when(center)(lambda: to_center().wait_send())
+            pl.when(jnp.logical_not(center))(lambda: to_inner().wait_send())
+            pl.when(jnp.logical_not(end))(lambda: to_outer().wait_send())
+
+        finish.append(done)
+
+    def g2(g):
+        clear_sums()
+        scale, offset = get(f"a1_{g}"), get(f"c1_{g}")
+        inverse, minus = get(f"r1_{g}"), get(f"m1_{g}")
+
+        def one(y, rows):
+            hidden = h2[g][rows, :]
+            pre = hidden * scale + offset
+            sig = logistic(pre)
+            grad = rx[g][rows, :].astype(jnp.float32) * (sig * (1.0 + pre * (1.0 - sig)))
+            h3[g][rows, :] = grad
+            add_sums(grad, grad * (hidden * inverse + minus))
+
+        lines(g, one)
+        send_sums(g * 6 + 4)
+
+    def d2(g):
+        back_vectors(g, 1, g * 6 + 4)
+        scale, k1, k0 = get(f"a1_{g}"), get(f"k11_{g}"), get(f"k01_{g}")
+        side = shape.maps[g]
+
+        def one(y, rows):
+            value = h3[g][rows, :] * scale + h2[g][rows, :] * k1 + k0
+            dpad[g][y + 1, pl.ds(1, side)] = value.astype(jnp.bfloat16).reshape(side, images, inner)
+
+        lines(g, one)
+
+    def sg(g):
+        side = shape.maps[g]
+        left = apad[g][pl.ds(1, side), pl.ds(1, side)].reshape(shape.rows[g], inner)
+        right = jnp.concatenate(
+            [
+                dpad[g][pl.ds(2 - i, side), pl.ds(2 - j, side), :, span(z, own, own)].reshape(
+                    shape.rows[g], own
+                )
+                for i in range(3)
+                for j in range(3)
+            ],
+            axis=1,
+        )
+        result = dot_tn(left, right)
+        for t in range(9):
+            part = result[:, t * own : (t + 1) * own].reshape(sacc.shape[1:])
+            sacc[t] = part if g == order[0] else sacc[t] + part
+
+    def f1b(g):
+        clear_sums()
+        scale, offset = get(f"a0_{g}"), get(f"c0_{g}")
+        inverse, minus = get(f"r0_{g}"), get(f"m0_{g}")
+
+        def slab(y, count, rows):
+            left = jnp.concatenate(windows(dpad[g], g, y, count), axis=1)
+            right = jnp.concatenate([swf[8 - t] for t in range(9)], axis=1)
+            h2[g][rows, :] = dot_nt(left, right)
+
+        slabs(g, slab)
+
+        def one(y, rows):
+            hidden = h1[g][rows, :]
+            pre = hidden * scale + offset
+            sig = logistic(pre)
+            grad = h2[g][rows, :] * (sig * (1.0 + pre * (1.0 - sig)))
+            h2[g][rows, :] = grad
+            add_sums(grad, grad * (hidden * inverse + minus))
+
+        lines(g, one)
+        send_sums(g * 6 + 5)
+
+    def d1(g):
+        back_vectors(g, 0, g * 6 + 5)
+        scale, k1, k0 = get(f"a0_{g}"), get(f"k10_{g}"), get(f"k00_{g}")
+
+        def one(y, rows):
+            value = h2[g][rows, :] * scale + h1[g][rows, :] * k1 + k0
+            xb[g][k_dh, rows, :] = value.astype(jnp.bfloat16)
+
+        lines(g, one)
+
+    def ig(g):
+        def slab(y, count, rows):
+            right = rwf[span(z, block, block), :]
+            h3[g][rows, :] = dot_nt(xb[g][k_dh, rows, :], right) + dz[g][rows, :].astype(
+                jnp.float32
+            )
+
+        slabs(g, slab)
+        start, wait = local(lambda: h3[g], lambda: i_out[g])
+        start()
+        finish.append(wait)
+
+    def rg(g):
+        result = dot_tn(xb[g][k_own], xb[g][k_dh])
+        for k in range(narrow):
+            part = result[:, k * own : (k + 1) * own].reshape(racc.shape[1:])
+            racc[k] = part if g == order[0] else racc[k] + part
+
+    class Total:
+        def __init__(self, acc, low, first, second, final, piece, out):
+            self.acc, self.low, self.first, self.second = acc, low, first, second
+            self.final, self.piece, self.out = final, piece, out
+            self.count = acc.shape[0]
+
+        def one(self):
+            def cast(a):
+                self.low[a] = self.acc[a, :, 1 - core].astype(jnp.bfloat16)
+
+            pl.loop(0, self.count)(cast)
+            start, self.got1 = remote(lambda: self.low, lambda: self.first, (sibling, z))
+            start()
+
+        def two(self):
+            self.got1()
+
+            def add(a):
+                self.first[a] = (
+                    self.first[a].astype(jnp.float32) + self.acc[a, :, core]
+                ).astype(jnp.bfloat16)
+
+            pl.loop(0, self.count)(add)
+            self.got2 = []
+            for j in range(1, chips):
+                peer = lax.rem(chip + j, chips)
+                start, wait = remote(
+                    lambda peer=peer: self.first.at[:, peer],
+                    lambda: self.second.at[chip],
+                    (peer * 2 + core, z),
+                )
+                start()
+                self.got2.append(wait)
+
+        def three(self):
+            for wait in self.got2:
+                wait()
+            self.second[chip] = self.first[:, chip]
+            target = self.final.at[:, chip, core] if self.piece is None else self.piece
+
+            def add(a):
+                total = self.second[0, a].astype(jnp.float32)
+                for k in range(1, chips):
+                    total = total + self.second[k, a].astype(jnp.float32)
+                target[a] = total.astype(jnp.bfloat16)
+
+            pl.loop(0, self.count)(add)
+            if self.piece is None:
+                self.send_pieces()
+                return
+            self.got3 = []
+            for k in range(1, narrow):
+                peer = lax.rem(z + k, narrow)
+                start, wait = remote(
+                    lambda peer=peer: self.piece.at[peer],
+                    lambda: self.final.at[z, chip, core],
+                    (w, peer),
+                )
+                start()
+                self.got3.append(wait)
+            self.final[z, chip, core] = self.piece[z]
+
+        def exchange(self):
+            for wait in self.got3:
+                wait()
+            self.send_pieces()
+
+        def send_pieces(self):
+            self.got4, self.got5 = [], []
+            for j in range(1, chips):
+                peer = lax.rem(chip + j, chips)
+                start, wait = remote(
+                    lambda: self.final.at[:, chip, core],
+                    lambda: self.final.at[:, chip, core],
+                    (peer * 2 + core, z),
+                )
+                start()
+                self.got4.append((j, wait))
+            start, wait = remote(
+                lambda: self.final.at[:, chip, core],
+                lambda: self.final.at[:, chip, core],
+                (sibling, z),
+            )
+            start()
+            self.got5.append(wait)
+
+        def four(self):
+            for j, arrived in self.got4:
+                arrived()
+                holder = lax.rem(chip + chips - j, chips)
+                start, wait = remote(
+                    lambda holder=holder: self.final.at[:, holder, core],
+                    lambda holder=holder: self.final.at[:, holder, core],
+                    (sibling, z),
+                )
+                start()
+                self.got5.append(wait)
+
+        def five(self):
+            for wait in self.got5:
+                wait()
+
+            def widen(a):
+                self.acc[a] = self.final[a].astype(jnp.float32)
+
+            pl.loop(0, self.count)(widen)
+            for source, target in self.out:
+                start, wait = local(source, target)
+                start()
+                finish.append(wait)
+
+    stotal = Total(sacc, sgb, sr1, sr2, sfin, None, [(lambda: sacc, lambda: sg_out)])
+    etotal = Total(
+        eacc,
+        egb,
+        er1,
+        er2,
+        efin,
+        epz,
+        [
+            (
+                lambda k=k: eacc.at[k],
+                lambda k=k: eg_out.at[:, :, :, pl.ds(k * block, block)],
+            )
+            for k in range(narrow)
+        ],
+    )
+    rtotal = Total(racc, rgb, rr1, rr2, rfin, rpz, [(lambda: racc, lambda: rg_out)])
+
+    def params():
+        for level, gain_out, shift_out in ((0, gg1, bg1), (1, gg2, bg2), (2, gg3, bg3)):
+            for kind, out in (("sg", gain_out), ("sb", shift_out)):
+                total = get(f"{kind}{level}_0") + get(f"{kind}{level}_1") + get(f"{kind}{level}_2")
+                if level == 2:
+                    out[...] = total
+                else:
+                    put("scratch", total)
+                    row = names["scratch"]
+                    out[...] = vec[row : row + 1, span(z, own, own)]
+
+    order = (0, 1, 2)
+
+    def weights_first():
+        for wait in own_waits:
+            wait()
+        rw_spread()
+        rw_cross()
+        rw_ready()
+
+    def expand_ready():
+        for wait in ew_waits:
+            wait()
+
+    plan = [
+        (weights_first,),
+        (f1, 0),
+        (sw_spread,),
+        (f1, 1),
+        (f1, 2),
+        (sw_cross,),
+        (a1, 0),
+        (sw_ready,),
+        (f2, 0),
+        (a1, 1),
+        (f2, 1),
+        (a2, 0),
+        (expand_ready,),
+        (f3, 0),
+        (a1, 2),
+        (a3, 0),
+        (a2, 1),
+        (f3, 1),
+        (b3, 0),
+        (za, 0, 0),
+        (f2, 2),
+        (a3, 1),
+        (zb, 0, 0),
+        (a2, 2),
+        (b3, 1),
+        (za, 1, 0),
+        (f3, 2),
+        (eg, 0),
+        (g2, 0),
+        (a3, 2),
+        (zb, 1, 0),
+        (d2, 0),
+        (b3, 2),
+        (za, 2, 0),
+        (za, 2, 1),
+        (za, 2, 2),
+        (f1b, 0),
+        (zb, 2, 0),
+        (sg, 0),
+        (zb, 2, 1),
+        (d1, 0),
+        (zb, 2, 2),
+        (eg, 1),
+        (eg, 2),
+        (etotal.one,),
+        (g2, 1),
+        (etotal.two,),
+        (ig, 0),
+        (rg, 0),
+        (d2, 1),
+        (etotal.three,),
+        (f1b, 1),
+        (etotal.exchange,),
+        (sg, 1),
+        (d1, 1),
+        (etotal.four,),
+        (ig, 1),
+        (rg, 1),
+        (etotal.five,),
+        (g2, 2),
+        (d2, 2),
+        (sg, 2),
+        (stotal.one,),
+        (f1b, 2),
+        (stotal.two,),
+        (d1, 2),
+        (rg, 2),
+        (rtotal.one,),
+        (stotal.three,),
+        (rtotal.two,),
+        (ig, 2),
+        (stotal.four,),
+        (rtotal.three,),
+        (stotal.five,),
+        (rtotal.exchange,),
+        (params,),
+        (rtotal.four,),
+        (rtotal.five,),
+    ]
+    for step, *arguments in plan:
+        step(*arguments)
+    for wait in finish:
+        wait()
+
+
+def kernel_call(shape, args):
+    inner, own, block, depth = shape.inner, shape.own, shape.block, shape.depth
+    wide, narrow, chips, images = shape.wide, shape.narrow, shape.chips, shape.images
+    bf16, f32 = jnp.bfloat16, jnp.float32
+
+    def struct(dims, kind):
+        return jax.ShapeDtypeStruct(dims, kind)
+
+    spread = [
+        (9, chips, 2, inner // wide, own),
+        (narrow, chips, 2, own // wide, block),
+        (narrow, chips, 2, block // wide, own),
+    ]
+    outs = (
+        [struct((rows, block), bf16) for rows in shape.rows]
+        + [struct((rows, block), f32) for rows in shape.rows]
+        + [struct(spread[2], f32), struct(spread[0], f32), struct((chips, 2, own // wide, depth), f32)]
+        + [struct((1, own), f32)] * 4
+        + [struct((1, block), f32)] * 2
+    )
+    anywhere = pl.BlockSpec(memory_space=pl.ANY)
+    vmem = pl.BlockSpec(memory_space=pltpu.VMEM)
+
+    def each_rows(columns, kind):
+        return [pltpu.VMEM((rows, columns), kind) for rows in shape.rows]
+
+    def padded():
+        return [pltpu.VMEM((side + 2, side + 2, images, inner), bf16) for side in shape.maps]
+
+    scratch = (
+        [pltpu.VMEM((narrow, rows, block), bf16) for rows in shape.rows]
+        + [
+            pltpu.VMEM((depth, inner), bf16),
+            pltpu.VMEM((9, inner, inner), bf16),
+            pltpu.VMEM((inner, block), bf16),
+        ]
+        + each_rows(inner, f32)
+        + each_rows(inner, f32)
+        + each_rows(block, f32)
+        + each_rows(block, bf16)
+        + padded()
+        + padded()
+        + each_rows(inner, bf16)
+        + each_rows(inner, bf16)
+        + [pltpu.VMEM(dims, f32) for dims in spread]
+        + [pltpu.VMEM((a, c, b, lanes), bf16) for a, c, _, b, lanes in spread]
+        + [pltpu.VMEM((a, c, b, lanes), bf16) for a, c, _, b, lanes in spread]
+        + [pltpu.VMEM((c, a, b, lanes), bf16) for a, c, _, b, lanes in spread]
+        + [pltpu.VMEM(dims, bf16) for dims in spread]
+        + [pltpu.VMEM((a, b, lanes), bf16) for a, _, _, b, lanes in spread[1:]]
+        + [
+            pltpu.VMEM((18, 2 * inner // 128, 128), f32),
+            pltpu.VMEM((18, wide, 2 * inner // 128, 128), f32),
+            pltpu.VMEM((8, inner), f32),
+            pltpu.VMEM((96, inner), f32),
+            pltpu.VMEM((narrow, 8, own), f32),
+            pltpu.SemaphoreType.DMA((SEMAPHORES,)),
+        ]
+    )
+    return pl.pallas_call(
+        functools.partial(block_kernel, shape),
+        out_shape=outs,
+        in_specs=[anywhere] * 9 + [vmem] * 6,
+        out_specs=[anywhere] * 9 + [vmem] * 6,
+        scratch_shapes=scratch,
+        compiler_params=pltpu.CompilerParams(
+            collective_id=0, has_side_effects=True, vmem_limit_bytes=VMEM_BYTES
+        ),
+        name="bottleneck",
+    )(*args)
+
+
+VMEM_BYTES = 66 * 1000 * 1000
+
+
+def kernel_body(shape, *arguments):
+    inputs, upstreams = arguments[:3], arguments[3:6]
+    reduce_weight, spatial_weight, expand_weight = arguments[6:9]
+    vectors = arguments[9:]
+
+    def flat(array):
+        return jnp.transpose(array, (1, 2, 0, 3)).reshape(-1, array.shape[3])
+
+    def unflat(array, side):
+        return jnp.transpose(
+            array.reshape(side, side, shape.images, array.shape[1]), (2, 0, 1, 3)
+        )
+
+    results = kernel_call(
+        shape,
+        [flat(x) for x in inputs]
+        + [flat(u) for u in upstreams]
+        + [
+            reduce_weight,
+            spatial_weight.reshape(9, shape.inner, shape.own),
+            expand_weight,
+        ]
+        + [v.reshape(1, -1) for v in vectors],
+    )
+    maps = list(shape.maps)
+    images = [unflat(r, side) for r, side in zip(results[:6], maps + maps)]
+    weights = [
+        results[6].reshape(reduce_weight.shape),
+        results[7].reshape(spatial_weight.shape),
+        results[8].reshape(expand_weight.shape),
+    ]
+    return tuple(images + weights + [r.reshape(-1) for r in results[9:]])
+
+
+def body(mesh, *arguments):
+    inputs, reduce_weight = arguments[0], arguments[6]
+    shape = Shape(
+        mesh,
+        [x.shape[1] for x in arguments[:3]],
+        inputs.shape[0],
+        inputs.shape[3],
+        arguments[8].shape[0] * mesh.shape["narrow"],
+    )
+    if shape.fits():
+        return kernel_body(shape, *arguments)
+    return plain_body(*arguments)
+
+
 def solution(mesh):
     rows = P("wide", None, None, None)
     blocks = P("wide", None, None, "narrow")
     weights = [P(None, "narrow"), P(None, None, None, "narrow"), P("narrow", None)]
     vectors = [P("narrow")] * 6
     return jax.shard_map(
-        plain_body,
+        functools.partial(body, mesh),
         mesh=mesh,
         in_specs=tuple([rows] * 3 + [blocks] * 3 + weights + vectors),
         out_specs=tuple([blocks] * 6 + weights + vectors),

time: 599 us -> 296 us (0.49)
  Pallas kernels: 0 us -> 277 us
  waiting for transfers between devices: 213 us -> 0 us
  blocking collectives: 178 us -> 0 us
  matrix products: 103 us -> 0 us
  other arithmetic: 55.5 us -> 0 us
  between operations: 14.8 us -> 0.71 us
  starting transfers between devices: 10.6 us -> 0 us
    pallas_call x0 -> x1, Pallas kernels: none -> 277 us  [kernel_call(): pl.pallas_call(functools.partial(block_kernel, shape), out_shape=outs, in...]
    psum x6 -> x0, blocking collectives: 141 us -> none  [the longest x1 25.7 us: plain_body(): sums1 = lax.psum(each(sums_forward, hidden1), 'wide')]
    psum x2 -> x0, waiting for transfers between devices: 122 us -> none  [the longest x1 73.5 us: plain_body(): lax.psum(dot('bhwd,id->bhwi', g, own_expand).astype(jnp.bfloat16), 'narrow')]
    dot_general x45 -> x0, matrix products: 69 us -> none  [the longest x18 49.8 us: dot(): return jnp.einsum(form, left, right, preferred_element_type=jnp.float32)]
    all_gather x2 -> x0, waiting for transfers between devices: 62.1 us -> none  [the longest x1 47.7 us: plain_body(): whole_spatial = lax.all_gather(spatial_weight, 'narrow', axis=3, tiled=True)]
    all_gather x1 -> x0, blocking collectives: 36.9 us -> none  [plain_body(): lax.all_gather(vectors, 'narrow', axis=1, tiled=True)]
    conv_general_dilated x6 -> x0, matrix products: 33.9 us -> none  [spatial(): lax.conv_general_dilated(inputs, kernel, (1, 1), ((1, 1), (1, 1)), dimens...]
    convert_element_type x17 -> x0, other arithmetic: 27.7 us -> none  [the longest x9 12 us: hidden_grad(): return (gain * inverse * (upstream - sums[0] / samples - normed * (sums[1...]
  transfers between devices with their start and end apart: 6 -> 0, of which waited for: 5 -> 0; matrix products, arithmetic and copies ran while one was open for 10% -> 0% of each run, Pallas kernels for 0% -> 0%
where the time goes in v2:
time: 296 us; the launch traced here: 295 us
  Pallas kernels  277 us (94%)
  local copies, waits for them, and re-layouts  17.9 us (6%)
    pallas_call x1, Pallas kernels, kernel_call(): pl.pallas_call(functools.partial(block_kernel, shape), out_shape=outs, in...  277 us
    unnamed x41, local copies, waits for them, and re-layouts  17.9 us

profile of v2, /device:TPU:0, one launch (start us, length us, event | category | flops | bytes accessed | tf_op | source)
XLA Modules:
  0.0 295.2 jit_solution(10648835967306906519)
XLA Ops:
  0.7 276.6 %bottleneck.1 = (bf16[400,512]{1,0:T(8,128)(2,1)}, bf16[784,512]{1,0:T(8,128)(2,1)}, bf16[1296,512]{1,0:T(8,128)(2,1)}, f32[400,512]{1,0:T(8,128)}, f32[784,512]...) custom-call(bf16[400,2048]{1,0:T(8,128)(2,1)} %bitcast.56, ...), custom_call_target="tpu_custom_call" | custom-call | tf_op jit(solution)/shard_map/bottleneck/pallas_call | solution.py:1179
  277.2 0.0 copy-start.3
  277.2 1.9 copy.45
  279.1 2.1 copy.46
  281.2 0.0 copy-done.3
  281.2 1.1 copy.47
  282.3 0.6 copy-done.6
  282.8 0.9 copy.48
  283.7 0.0 copy-done.2
  283.7 1.2 copy.49
  284.9 1.2 copy-done
  286.0 1.5 copy.50
  287.6 0.5 copy-done.5
  288.0 1.0 copy.51
  289.0 0.0 copy-done.1
  289.0 1.4 copy.52
  290.4 0.6 copy-done.4
  291.0 0.0 copy-start.8
  291.0 0.0 copy-start.7
  291.0 1.0 copy.53
  292.0 0.0 copy-done.12
  292.0 0.5 copy.54
  292.5 0.0 copy-done.11
  292.5 0.5 copy.55
  293.0 0.0 copy-done.10
  293.0 0.5 copy.56
  293.5 0.0 copy-done.9
  293.5 0.5 copy.57
  294.0 0.0 copy-done.8
  294.0 0.6 copy.58
  294.6 0.0 copy-done.7
  294.6 0.6 copy.59
  (10 shorter events, 0.0 us)
Async XLA Ops:
  277.2 4.0 %copy-start.3 = (bf16[1296,512]{1,0:T(8,128)(2,1)S(1)}, bf16[1296,512]{1,0:T(8,128)(2,1)}, u32[]{:S(2)}) copy-start(bf16[1296,512]{1,0:T(8,128)(2,1)} %get-tuple-element.32) | copy-start | bytes 3981316
  281.2 1.6 copy-start.6
  281.2 2.5 copy-start.2
  283.7 2.3 copy-start
  286.0 2.0 copy-start.5
  286.0 3.0 %copy-start.1 = (f32[9,4,2,64,128]{4,3,2,1,0:T(8,128)S(1)}, f32[9,4,2,64,128]{4,3,2,1,0:T(8,128)}, u32[]{:S(2)}) copy-start(f32[9,4,2,64,128]{4,3,2,1,0:T(8,128)} %get-tuple-element.37) | copy-start | bytes 7077892
  289.0 2.0 copy-start.4
  291.0 1.0 copy-start.12
  291.0 1.5 copy-start.11
  291.0 2.0 copy-start.10
  291.0 2.5 copy-start.9
  291.0 3.1 %copy-start.8 = (f32[1,512]{1,0:T(1,128)S(1)}, f32[1,512]{1,0:T(1,128)}, u32[]{:S(2)}) copy-start(f32[1,512]{1,0:T(1,128)} %get-tuple-element.43) | copy-start | bytes 6148
  291.0 3.6 %copy-start.7 = (f32[1,512]{1,0:T(1,128)S(1)}, f32[1,512]{1,0:T(1,128)}, u32[]{:S(2)}) copy-start(f32[1,512]{1,0:T(1,128)} %get-tuple-element.44) | copy-start | bytes 6148
